TPU v7x, 128 devices: a whole 4x4x4 slice. The times are simulated.
128 devices in a mesh: tp: 16 (over z, x_lo, core), dp: 8 (over x_hi, y).
Axes of the slice: x: 4 (x_hi: 2, x_lo: 2; x = x_hi * 2 + x_lo), y: 4, z: 4, core: 2. Of those that a mesh axis runs over, the one named last changes fastest.
Arguments:
- hidden_in: bfloat16 [16384, 7168], P(('dp', 'tp')), may hold values from -6 to 6
- norm_gain: float32 [7168], replicated, may hold values from 0.25 to 1.75
- w_qkv: bfloat16 [3, 7168, 4096], P(None, None, 'tp')
- w_out: bfloat16 [4096, 3584], P('tp'), may hold values from -0.1875 to 0.1875
- lengths: int32 [16], replicated, may hold values from 256 to 1024, as said below
- student_in: bfloat16 [16384, 1024], P(('dp', 'tp')), may hold values from -6 to 6
- student_gain: float32 [1024], replicated, may hold values from 0.25 to 1.75
- proj_weight: bfloat16 [3584, 1024], P('tp'), may hold values from -0.1875 to 0.1875
- loss_scale: float32 [1], replicated, may hold values from 32768 to 131072
Outputs:
- student_grad: bfloat16 [16384, 1024], P(('dp', 'tp'))
- proj_grad: bfloat16 [3584, 1024], P('tp')
- gain_grad: float32 [1024], replicated
- loss: float32 [], replicated
Inputs may be any that keep to these rules, and one draw needn't show every extreme that they name: One of the lengths equals 1024.
All inputs are finite; a program needn't handle non-finite values.
Results may differ from a plain program's by a relative error of at most 0.02.
Values may be sent and summed in bfloat16 or wider, within the bound.
A program may use at most 192 MiB of HBM per device.

v0:
```python
import math

import jax
import jax.numpy as jnp
from jax import lax
from jax.sharding import PartitionSpec as P

HEAD = 128
HW = 3584
LEN = 1024
SEQS = 2


def layer_norm(rows, gain):
    values = rows.astype(jnp.float32)
    centred = values - jnp.mean(values, axis=-1, keepdims=True)
    spread = jnp.mean(centred * centred, axis=-1, keepdims=True)
    return (centred * lax.rsqrt(spread + 1e-05) * gain).astype(jnp.bfloat16)


def rms_norm(rows, gain):
    return rows * lax.rsqrt(jnp.mean(rows * rows, axis=-1, keepdims=True) + 1e-06) * gain


def valid_rows(first_row, count, group_lengths):
    rows = first_row + jnp.arange(count, dtype=jnp.int32)
    caption = rows // LEN
    position = rows % LEN
    picked = jnp.where(
        caption[:, None] == jnp.arange(SEQS, dtype=jnp.int32)[None, :], group_lengths[None, :], 0
    )
    return position < jnp.sum(picked, axis=1)


def single_caption(inputs):
    query, keys, values, length = inputs
    scores = jnp.einsum("qhd,khd->hqk", query, keys, preferred_element_type=jnp.float32) * (
        1.0 / math.sqrt(HEAD)
    )
    position = jnp.arange(LEN, dtype=jnp.int32)
    allowed = (position[None, :] <= position[:, None]) & (position[None, :] < length)
    scores = jnp.where(allowed[None], scores, -1e30)
    weights = jnp.exp(scores - jnp.max(scores, axis=-1, keepdims=True))
    probs = (weights / jnp.sum(weights, axis=-1, keepdims=True)).astype(jnp.bfloat16)
    return jnp.einsum("hqk,khd->qhd", probs, values, preferred_element_type=jnp.float32).astype(
        jnp.bfloat16
    )


def attend(projected, group_lengths):
    width = projected.shape[2]
    total = projected.shape[1]
    shaped = projected.reshape(3, SEQS, LEN, width // HEAD, HEAD)
    context = lax.map(single_caption, (shaped[0], shaped[1], shaped[2], group_lengths))
    return context.reshape(total, width)


def shards(
    hidden_in, norm_gain, w_qkv, w_out, lengths, student_in, student_gain, proj_weight, loss_scale
):
    rows_dev = hidden_in.shape[0]
    tp_place = lax.axis_index("tp")
    group = lax.axis_index("dp")
    group_lengths = lax.dynamic_slice_in_dim(lengths, group * SEQS, SEQS)
    count = jnp.sum(lengths).astype(jnp.float32)
    factor = 2.0 * loss_scale[0] / (count * HW)
    own_rows = student_in.astype(jnp.float32)
    normed_local = layer_norm(hidden_in, norm_gain)
    projected = jnp.einsum(
        "td,kdf->ktf",
        lax.all_gather(normed_local, "tp", axis=0, tiled=True),
        w_qkv,
        preferred_element_type=jnp.float32,
    ).astype(jnp.bfloat16)
    context = attend(projected, group_lengths)
    block = context
    mixed = lax.psum_scatter(
        jnp.dot(block, w_out, preferred_element_type=jnp.float32).astype(jnp.bfloat16),
        "tp",
        scatter_dimension=0,
        tiled=True,
    ).astype(jnp.float32)
    target = (hidden_in[:, :HW].astype(jnp.float32) + mixed).astype(jnp.bfloat16)
    proj_whole = lax.all_gather(proj_weight, "tp", axis=0, tiled=True)
    student_norm = rms_norm(own_rows, student_gain).astype(jnp.bfloat16)
    mapped = lax.dot_general(
        student_norm, proj_whole, (((1,), (1,)), ((), ())), preferred_element_type=jnp.float32
    )
    valid = valid_rows(tp_place * rows_dev, rows_dev, group_lengths)
    diff = jnp.where(valid[:, None], mapped - target.astype(jnp.float32), 0.0)
    loss_part = jnp.sum(diff * diff)
    delta = (diff * factor).astype(jnp.bfloat16)
    norm_back = jnp.dot(delta, proj_whole, preferred_element_type=jnp.float32)
    block = delta
    proj_part = lax.psum_scatter(
        lax.dot_general(
            block, student_norm, (((0,), (0,)), ((), ())), preferred_element_type=jnp.float32
        ).astype(jnp.bfloat16),
        "tp",
        scatter_dimension=0,
        tiled=True,
    )
    proj_total = lax.psum(proj_part, "dp").astype(jnp.float32)
    unused, pull_back = jax.vjp(rms_norm, own_rows, student_gain)
    row_grad, gain_part = pull_back(norm_back)
    loss_total, gain_total = lax.psum((loss_part, gain_part), ("tp", "dp"))
    return (
        row_grad.astype(jnp.bfloat16),
        proj_total.astype(jnp.bfloat16),
        gain_total,
        loss_total / (count * HW),
    )


def solution(mesh):
    placed = (
        P(("dp", "tp"), None),
        P(),
        P(None, None, "tp"),
        P("tp", None),
        P(),
        P(("dp", "tp"), None),
        P(),
        P("tp", None),
        P(),
    )
    return jax.shard_map(
        shards,
        mesh=mesh,
        in_specs=placed,
        out_specs=(P(("dp", "tp"), None), P("tp", None), P(), P()),
        check_vma=False,
    )
```

profile of v0, /device:TPU:1, one launch (start us, length us, event | category | flops | bytes accessed | tf_op | source)
XLA Modules:
  0.0 605.7 jit_solution(15004335973062452192)
XLA Ops:
  7.2 2.0 convert_reduce_fusion
  9.2 2.1 fusion.20
  11.4 1.9 fusion.22
  14.2 153.8 %all-gather.5.cloned.1.call-done = bf16[2048,7168]{1,0:T(8,128)(2,1)} async-done(((bf16[128,7168]{1,0:T(8,128)(2,1)}), bf16[2048,7168]{1,0:T(8,128)(2,1)}) %all-gather.5.cloned.1.call-update) | async-done | bytes 29360144 | tf_op jit(solution)/shard_map/all_gather | solution.py:71
  168.1 29.6 %fusion.26 = bf16[3,2048,256]{2,1,0:T(8,128)(2,1)S(1)} fusion(bf16[3,7168,256]{2,1,0:T(8,128)(2,1)} %param.13, bf16[2048,7168]{1,0:T(8,128)(2,1)} %all-gather.5.cloned.1.call-done), kind=kOutput, calls=%fused_computation.39 | convolution fusion | flops 22550151168 | bytes 43515904 | tf_op jit(solution)/shard_map/td,kdf->ktf/dot_general | solution.py:69
  197.7 1.5 fusion.45
  199.2 2.3 squeeze.24
  201.5 2.2 squeeze.25
  204.7 38.8 %while.10 = (s32[]{:T(128)}, bf16[2,1024,2,128]{3,2,1,0:T(2,128)(2,1)}, bf16[2,1024,2,128]{3,2,1,0:T(2,128)(2,1)}, s32[2]{0:T(128)S(1)}, bf16[2,1024,2,128]{3,2,...) while((s32[]{:T(128)}, bf16[2,1024,2,128]{3,2,1,0:T(2,128)(2,1)}, ...), condition=%wide.region_7.8_spmd, body=%wide.region_4.0_spmd.sunk | while | flops 1088686080 | bytes 27282020 | solution.py:54
  204.7 2.7 constant_dynamic-slice_fusion.5
  209.0 7.6 %fusion.56 = (f32[2,1024]{1,0:T(2,128)S(1)}, f32[2,1024,1024]{1,2,0:T(8,128)}) fusion(pred[1024,1024]{0,1:T(8,128)(4,1)S(1)} %fusion.55, bf16[1,1024,2,128]{3,2,1,0:T(2,128)(2,1)} %get-tuple-element.122, bf16[1,1024,2,128]{3,2,1,0:T(2,128)(2,1)S(1)} %get-tuple-element.123), kind=kOutput, calls=%fused_computation.72.clone.1 | convolution fusion | flops 545260544 | bytes 10493952 | tf_op jit(solution)/shard_map/while/body/eval_jaxpr/sub | solution.py:43
  218.4 4.1 fusion.57
  224.2 2.7 constant_dynamic-slice_fusion.5
  228.5 7.5 %fusion.56 = (f32[2,1024]{1,0:T(2,128)S(1)}, f32[2,1024,1024]{1,2,0:T(8,128)}) fusion(pred[1024,1024]{0,1:T(8,128)(4,1)S(1)} %fusion.55, bf16[1,1024,2,128]{3,2,1,0:T(2,128)(2,1)} %get-tuple-element.122, bf16[1,1024,2,128]{3,2,1,0:T(2,128)(2,1)S(1)} %get-tuple-element.123), kind=kOutput, calls=%fused_computation.72.clone.1 | convolution fusion | flops 545260544 | bytes 10493952 | tf_op jit(solution)/shard_map/while/body/eval_jaxpr/sub | solution.py:43
  237.8 4.1 fusion.57
  243.5 8.5 %convolution_convert_fusion = bf16[2048,3584]{1,0:T(8,128)(2,1)} fusion(bf16[256,3584]{1,0:T(8,128)(2,1)S(1)} %copy-done, bf16[256,8,2,128]{3,2,1,0:T(2,128)(2,1)} %bitcast.59), kind=kOutput, calls=%fused_computation.27 | convolution fusion | flops 3765436416 | bytes 17563648 | tf_op jit(solution)/shard_map/dot_general | solution.py:78
  254.4 157.9 %reduce-scatter.3.cloned.1.call-done = bf16[128,3584]{1,0:T(8,128)(2,1)} async-done(((bf16[2048,3584]{1,0:T(8,128)(2,1)}), bf16[128,3584]{1,0:T(8,128)(2,1)}) %reduce-scatter.3.cloned.1.call-update) | async-done | bytes 917520 | tf_op jit(solution)/shard_map/reduce_scatter | solution.py:77
  412.3 6.9 %multiply_reduce_fusion = (f32[]{:T(128)}, f32[128,3584]{1,0:T(8,128)S(1)}) fusion(bf16[128,3584]{1,0:T(8,128)(2,1)} %reduce-scatter.3.cloned.1.call-done, bf16[128,7168]{1,0:T(8,128)(2,1)} %param.11, bf16[3584,1024]{1,0:T(8,128)(2,1)} %all-gather.3.cloned.1.call-done, bf16[128,1024]{1,0:T(8,128)(2,1)S(1)} %copy-done.3, f32[1024]{0:T(1024)S(1)} %copy-done.4, ...), kind=kOutput, calls=%fused_computation.40 | convolution fusion | flops 944177152 | bytes 11276932 | tf_op jit(solution)/shard_map/dot_general | solution.py:86
  420.5 5.1 convolution_convert_fusion.1
  425.7 4.9 fusion.34
  430.6 66.7 %all-reduce = (f32[1024]{0:T(1024)}, f32[]{:T(128)}) all-reduce(f32[1024]{0:T(1024)S(1)} %get-tuple-element.55, f32[]{:T(128)} %get-tuple-element.79), channel_id=1, replica_groups=mesh['tp'=16,'dp'=8] {'tp','dp'}, use_global_device_ids=true, to_apply=%region_14.15 | all-reduce | flops 1025 | bytes 8200 | tf_op jit(solution)/shard_map/psum | solution.py:106
  498.0 15.2 %reduce-scatter.5.cloned.1.call-done = bf16[224,1024]{1,0:T(8,128)(2,1)} async-done(((bf16[3584,1024]{1,0:T(8,128)(2,1)}), bf16[224,1024]{1,0:T(8,128)(2,1)}) %reduce-scatter.5.cloned.1.call-update) | async-done | bytes 458768 | tf_op jit(solution)/shard_map/reduce_scatter | solution.py:95
  514.1 82.1 %all-reduce.3.cloned.1.call-done = bf16[224,1024]{1,0:T(8,128)(2,1)} async-done(((bf16[224,1024]{1,0:T(8,128)(2,1)}), bf16[224,1024]{1,0:T(8,128)(2,1)}) %all-reduce.3.cloned.1.call-update) | async-done | bytes 458768 | tf_op jit(solution)/shard_map/psum | solution.py:103
  596.2 1.8 copy.75
  (52 shorter events, 15.3 us)
Async XLA Ops:
  7.2 236.4 %copy-start = (bf16[256,3584]{1,0:T(8,128)(2,1)S(1)}, bf16[256,3584]{1,0:T(8,128)(2,1)}, u32[]{:S(2)}) copy-start(bf16[256,3584]{1,0:T(8,128)(2,1)} %param.14) | copy-start | bytes 5505028
  7.2 4.2 copy-start.5
  7.2 160.9 %all-gather.5.cloned.1.call-start = ((), (), s32[]{:S(2)}) async-start(), calls=%async_computation.3 | async-start | bytes 31195136 | tf_op jit(solution)/shard_map/all_gather | solution.py:71
  7.2 4.2 copy-start.2
  9.2 4.9 copy-start.6
  13.3 241.0 %all-gather.3.cloned.1.call-start = ((), (), s32[]{:S(2)}) async-start(), calls=%async_computation.2 | async-start | bytes 7798784 | tf_op jit(solution)/shard_map/all_gather | solution.py:84
  14.1 398.2 %reduce-scatter.3.cloned.1.call-start = ((), (), s32[]{:S(2)}) async-start(), calls=%async_computation.4 | async-start | bytes 15597568 | tf_op jit(solution)/shard_map/reduce_scatter | solution.py:77
  252.0 2.2 copy-start.3
  252.0 160.2 %copy-start.4 = (f32[1024]{0:T(1024)S(1)}, f32[1024]{0:T(1024)}, u32[]{:S(2)}) copy-start(f32[1024]{0:T(1024)} %param.17) | copy-start | bytes 12292
  252.1 261.1 %reduce-scatter.5.cloned.1.call-start = ((), (), s32[]{:S(2)}) async-start(), calls=%async_computation.5 | async-start | bytes 7798784 | tf_op jit(solution)/shard_map/reduce_scatter | solution.py:95
  419.2 1.3 copy-start.1
  425.6 170.6 %all-reduce.3.cloned.1.call-start = ((), (), s32[]{:S(2)}) async-start(), calls=%async_computation.6 | async-start | bytes 917504 | tf_op jit(solution)/shard_map/psum | solution.py:103
Sparse Core Ops, SparseCore 0:
  13.5 154.5 all-gather.4
  169.8 48.1 all-gather.2
  252.2 160.0 reduce-scatter.2
  425.8 87.3 reduce-scatter.4
  515.5 80.6 all-reduce.2
where the time goes:
time: 611 us; the launch traced here: 606 us
  waiting for transfers between devices  410 us (67%)
  matrix products  78.3 us (13%)
  blocking collectives  66.7 us (11%)
  local copies, waits for them, and re-layouts  23.7 us (4%)
  between operations  17 us (3%)
  other arithmetic  9.81 us (2%)
    reduce_scatter x1, waiting for transfers between devices, shards(): lax.psum_scatter(jnp.dot(block, w_out, preferred_element_type=jnp.float32...  158 us
    all_gather x1, waiting for transfers between devices, shards(): lax.all_gather(normed_local, 'tp', axis=0, tiled=True)  154 us
    psum x1, waiting for transfers between devices, shards(): proj_total = lax.psum(proj_part, 'dp').astype(jnp.float32)  82.1 us
    psum x1, blocking collectives, shards(): loss_total, gain_total = lax.psum((loss_part, gain_part), ('tp', 'dp'))  66.7 us
    dot_general x1, matrix products, shards(): jnp.einsum('td,kdf->ktf', lax.all_gather(normed_local, 'tp', axis=0, tile...  29.6 us
    reduce_scatter x1, waiting for transfers between devices, shards(): lax.psum_scatter(lax.dot_general(block, student_norm, (((0,), (0,)), ((),...  15.2 us
    sub x2, matrix products, single_caption(): weights = jnp.exp(scores - jnp.max(scores, axis=-1, keepdims=True))  15.1 us
  transfers between devices with their start and end apart: 5, of which 4 were waited for; matrix products, arithmetic and copies ran while one was open for 15% of the time, Pallas kernels for 0%

commit v1 on v0

v1 whole, which is shorter than its diff:
```python
import functools
import math

import jax
import jax.numpy as jnp
from jax import lax
from jax.experimental import pallas as pl
from jax.experimental.pallas import tpu as pltpu
from jax.sharding import PartitionSpec as P

HEAD = 128
HW = 3584
LEN = 1024
SEQS = 2
D = 7168
ROWS = 128
FIRST = 80
MESH = pl.DeviceIdType.MESH
MIB = 1 << 20


def place():
    tp = lax.axis_index("tp")
    return tp // 4, (tp // 2) % 2, tp % 2


def at(z, x, core):
    return {"tp": (z % 4) * 4 + x * 2 + core}


def across(z, x, core):
    dp = lax.axis_index("dp")
    return {"tp": z * 4 + (1 - x) * 2 + core, "dp": (1 - dp // 4) * 4 + dp % 4}


def remote(src, dst, send, recv, device):
    return pltpu.make_async_remote_copy(
        src_ref=src, dst_ref=dst, send_sem=send, recv_sem=recv, device_id=device, device_id_type=MESH
    )


def greet(devices):
    barrier = pltpu.get_barrier_semaphore()
    for device in devices:
        pl.semaphore_signal(barrier, 1, device_id=device, device_id_type=MESH)
    pl.semaphore_wait(barrier, len(devices))


def project_kernel(
    x_ref, gain_ref, w_hbm, wout_hbm, qkv_ref, wout_all, normed, rows, w, send, recv, wsend, wrecv, local
):
    z, x, core = place()
    other = 1 - x
    kept = z // 2
    rel = (z - 2 * core + 4) % 4
    ahead = (rel == 0) | (rel == 3)
    step = jnp.where(ahead, 1, -1)
    near = (z + step + 4) % 4
    onward = (z - step + 4) % 4
    via = jnp.where(ahead, 1, 0)
    far = (z + 2) % 4

    greet(
        [at(z, x, 1 - core)]
        + [at(zz, x, c) for zz in (z + 1, z + 3) for c in (0, 1)]
        + [at(z, other, c) for c in (0, 1)]
        + [across(z, x, c) for c in (0, 1)]
    )

    w_out_going = [
        remote(w_hbm.at[k], w.at[core, k], wsend.at[k], wrecv.at[k], at(z, x, 1 - core)) for k in range(3)
    ]
    w_own = [pltpu.make_async_copy(w_hbm.at[k], w.at[core, k], local.at[k]) for k in range(3)]
    slot = x * 2 + core
    proj_going = [
        remote(wout_hbm, wout_all.at[slot], wsend.at[3], wrecv.at[3 + core], at(z, x, 1 - core)),
        remote(wout_hbm, wout_all.at[slot], wsend.at[4], wrecv.at[5 + core], across(z, x, 0)),
        remote(wout_hbm, wout_all.at[slot], wsend.at[5], wrecv.at[5 + core], across(z, x, 1)),
    ]
    proj_own = pltpu.make_async_copy(wout_hbm, wout_all.at[slot], local.at[3])
    for copy in w_own + w_out_going + proj_going + [proj_own]:
        copy.start()

    def part(chunk_z, chunk_x, s, cls):
        chunk = (chunk_z % 2) * 2 + chunk_x
        start, size = ((0, FIRST), (FIRST, ROWS - FIRST))[cls]
        return rows.at[chunk, pl.ds(pl.multiple_of(s * ROWS + start, 16), size)]

    def sem(chunk_z, chunk_x, s, cls):
        return recv.at[((chunk_z % 2) * 2 + chunk_x) * 4 + s * 2 + cls]

    def arrived(chunk_z, chunk_x, s, cls):
        ref = part(chunk_z, chunk_x, s, cls)
        remote(ref, ref, send.at[0], sem(chunk_z, chunk_x, s, cls), at(z, x, 1 - core)).wait_recv()

    def forward(chunk_z, chunk_x, s, cls, index, device):
        ref = part(chunk_z, chunk_x, s, cls)
        return remote(ref, ref, send.at[index], sem(chunk_z, chunk_x, s, cls), device)

    def norm(start, size):
        def one(i, carry):
            block = pl.ds(pl.multiple_of(start + i * 16, 16), 16)
            values = x_ref[block, :].astype(jnp.float32)
            centred = values - jnp.mean(values, axis=-1, keepdims=True)
            spread = jnp.mean(centred * centred, axis=-1, keepdims=True)
            normed[block, :] = (centred * lax.rsqrt(spread + 1e-05) * gain_ref[...]).astype(jnp.bfloat16)
            return carry

        lax.fori_loop(0, size // 16, one, 0)

    def own_copies(cls):
        start, size = ((0, FIRST), (FIRST, ROWS - FIRST))[cls]
        src = normed.at[pl.ds(start, size)]
        dst = part(z, x, core, cls)
        got = sem(z, x, core, cls)
        base = cls * 4
        return (
            [
                remote(src, dst, send.at[base], got, at(z + 1, x, kept)),
                remote(src, dst, send.at[base + 1], got, at(z + 3, x, kept)),
                remote(src, dst, send.at[base + 2], got, at(z, other, kept)),
            ],
            remote(src, dst, send.at[base + 3], got, at(z, x, 1 - core)),
            pltpu.make_async_copy(src, dst, local.at[4 + cls]),
        )

    for cls, (start, size) in ((1, (FIRST, ROWS - FIRST)), (0, (0, FIRST))):
        norm(start, size)
        away, sibling, here = own_copies(cls)
        for copy in away:
            copy.start()

        @pl.when(core == kept)
        def _():
            here.start()

        @pl.when(core != kept)
        def _():
            sibling.start()

    def multiply(chunk_z, chunk_x):
        chunk = (chunk_z % 2) * 2 + chunk_x

        def one(n, carry):
            out = jnp.dot(rows[chunk], w[n % 2, n // 2], preferred_element_type=jnp.float32)
            qkv_ref[n, pl.ds(pl.multiple_of(chunk * 256, 256), 256), :] = out.astype(jnp.bfloat16)
            return carry

        lax.fori_loop(0, 6, one, 0)

    source = rel < 2

    fx = []
    for s in (0, 1):
        arrived(near, x, s, 1)
        fx.append(forward(near, x, s, 1, 8 + s, at(z, other, core)))
        fx[-1].start()
    on_b = forward(near, x, via, 1, 10, at(onward, x, core))
    on_b.start()

    for copy in w_own:
        copy.wait()
    for k in range(3):
        remote(w_hbm.at[k], w.at[1 - core, k], wsend.at[k], wrecv.at[k], at(z, x, 1 - core)).wait_recv()

    @pl.when(source)
    def _():
        for cls in (0, 1):
            arrived(z, x, 1 - core, cls)
            own_copies(cls)[2].wait()
        multiply(z, x)

    for s in (0, 1):
        arrived(near, x, s, 0)
    on_a = forward(near, x, via, 0, 11, at(onward, x, core))
    on_a.start()

    def spread():
        return [
            forward(z, other, s, 0, 12 + s * 2 + i, at(zz, x, core))
            for s in (0, 1)
            for i, zz in enumerate((z + 1, z + 3))
        ]

    def crossing():
        return [forward(far, x, s, 1, 12 + s, at(z, other, core)) for s in (0, 1)]

    @pl.when(source)
    def _():
        for s in (0, 1):
            arrived(z, other, s, 0)
        for copy in spread():
            copy.start()
        for s in (0, 1):
            arrived(z, other, s, 1)
        multiply(z, other)

    @pl.when(jnp.logical_not(source))
    def _():
        for s in (0, 1):
            arrived(far, x, s, 1)
        for copy in crossing():
            copy.start()
        multiply(near, x)

    for s in (0, 1):
        arrived(near, other, s, 0)
    on_p = forward(near, other, via, 0, 16, at(onward, x, core))
    on_p.start()

    @pl.when(source)
    def _():
        multiply(near, x)

    for s in (0, 1):
        arrived(near, other, s, 1)
    multiply(near, other)

    @pl.when(jnp.logical_not(source))
    def _():
        for s in (0, 1):
            arrived(far, x, s, 0)
        multiply(far, x)
        for s in (0, 1):
            arrived(far, other, s, 0)
            arrived(far, other, s, 1)
        multiply(far, other)

    for cls in (0, 1):
        away, sibling, here = own_copies(cls)
        for copy in away:
            copy.wait_send()

        @pl.when(core != kept)
        def _():
            sibling.wait_send()

    for copy in fx + [on_b, on_a, on_p]:
        copy.wait_send()

    @pl.when(source)
    def _():
        for copy in spread():
            copy.wait_send()

    @pl.when(jnp.logical_not(source))
    def _():
        for copy in crossing():
            copy.wait_send()

    for copy in w_out_going + proj_going:
        copy.wait_send()
    proj_own.wait()
    remote(
        wout_hbm, wout_all.at[x * 2 + 1 - core], wsend.at[3], wrecv.at[3 + 1 - core], at(z, x, 1 - core)
    ).wait_recv()
    for c in (0, 1):
        remote(wout_hbm, wout_all.at[other * 2 + c], wsend.at[4], wrecv.at[5 + c], across(z, x, c)).wait_recv()


def project(hidden, gain, w_qkv, w_out):
    return pl.pallas_call(
        project_kernel,
        name="project",
        out_shape=(
            jax.ShapeDtypeStruct((6, LEN, 256), jnp.bfloat16),
            jax.ShapeDtypeStruct((4, 256, HW), jnp.bfloat16),
        ),
        in_specs=[
            pl.BlockSpec(memory_space=pltpu.VMEM),
            pl.BlockSpec(memory_space=pltpu.VMEM),
            pl.BlockSpec(memory_space=pltpu.HBM),
            pl.BlockSpec(memory_space=pltpu.HBM),
        ],
        out_specs=(pl.BlockSpec(memory_space=pltpu.VMEM), pl.BlockSpec(memory_space=pltpu.HBM)),
        scratch_shapes=[
            pltpu.VMEM((ROWS, D), jnp.bfloat16),
            pltpu.VMEM((4, 2 * ROWS, D), jnp.bfloat16),
            pltpu.VMEM((2, 3, D, 256), jnp.bfloat16),
            pltpu.SemaphoreType.DMA((17,)),
            pltpu.SemaphoreType.DMA((16,)),
            pltpu.SemaphoreType.DMA((6,)),
            pltpu.SemaphoreType.DMA((7,)),
            pltpu.SemaphoreType.DMA((6,)),
        ],
        compiler_params=pltpu.CompilerParams(
            collective_id=0, has_side_effects=True, vmem_limit_bytes=60 * MIB
        ),
    )(hidden, gain, w_qkv, w_out)


def attend_kernel(
    len_ref, qkv_ref, wout_ref, hid_hbm, target_ref, hid_ref, ctx, ctx_in, stage, parts, send, recv, osend, orecv, local
):
    z, x, core = place()
    other = 1 - x
    kept = z // 2
    length = len_ref[0]
    fetch = pltpu.make_async_copy(hid_hbm.at[:, pl.ds(0, HW)], hid_ref, local)
    fetch.start()

    greet(
        [at(z, x, 1 - core)]
        + [at(zz, x, c) for zz in (z + 1, z + 2, z + 3) for c in (0, 1)]
        + [at(z, other, core)]
    )

    def attend(chunk, keys, zq, mine):
        start = pl.multiple_of(chunk * 256, 256)
        row = lax.broadcasted_iota(jnp.int32, (256, keys), 0) + start
        col = lax.broadcasted_iota(jnp.int32, (256, keys), 1)
        allowed = (col <= row) & (col < length)

        def pair(half, carry):
            for h in (0, 1):
                lanes = slice(h * HEAD, (h + 1) * HEAD)
                q = qkv_ref[half, pl.ds(start, 256), lanes]
                k = qkv_ref[2 + half, :keys, lanes]
                v = qkv_ref[4 + half, :keys, lanes]
                scores = lax.dot_general(
                    q, k, (((1,), (1,)), ((), ())), preferred_element_type=jnp.float32
                ) * (1.0 / math.sqrt(HEAD))
                scores = jnp.where(allowed, scores, -1e30)
                weights = jnp.exp(scores - jnp.max(scores, axis=-1, keepdims=True))
                total = jnp.sum(weights, axis=-1, keepdims=True)
                out = jnp.dot(weights.astype(jnp.bfloat16), v, preferred_element_type=jnp.float32)
                ctx[zq * 2 + mine, half, :, lanes] = (out / total).astype(jnp.bfloat16)
            return carry

        lax.fori_loop(0, 2, pair, 0)

    def swap(zq):
        return remote(ctx.at[zq * 2], ctx_in.at[zq], send.at[zq], recv.at[zq], at(z, other, core))

    def give(zq, s):
        return remote(
            stage.at[zq, pl.ds(s * ROWS, ROWS)],
            parts.at[z],
            osend.at[zq * 2 + s],
            orecv.at[z],
            at(2 * core + zq, x, s),
        )

    def keep(zq, s):
        return pltpu.make_async_copy(stage.at[zq, pl.ds(s * ROWS, ROWS)], parts.at[z], osend.at[zq * 2 + s])

    for zq in (0, 1):
        keys = (zq + 1) * 512
        attend(zq * 2 + other, keys, zq, 0)
        swap(zq).start()
        attend(zq * 2 + x, keys, zq, 1)
        swap(zq).wait_recv()

        def one(n, carry):
            lanes = pl.ds(pl.multiple_of(n * 512, 512), 512)
            out = jnp.zeros((256, 512), jnp.float32)
            for half in (0, 1):
                out += jnp.dot(
                    ctx[zq * 2 + 1, half], wout_ref[x * 2 + half, :, lanes], preferred_element_type=jnp.float32
                )
                out += jnp.dot(
                    ctx_in[zq, half], wout_ref[other * 2 + half, :, lanes], preferred_element_type=jnp.float32
                )
            stage[zq, :, lanes] = out.astype(jnp.bfloat16)
            return carry

        lax.fori_loop(0, HW // 512, one, 0)
        for s in (0, 1):
            mine = (2 * core + zq == z) & (core == s)

            @pl.when(mine)
            def _():
                keep(zq, s).start()

            @pl.when(jnp.logical_not(mine))
            def _():
                give(zq, s).start()

    for zq in (0, 1):
        swap(zq).wait_send()
        for s in (0, 1):
            mine = (2 * core + zq == z) & (core == s)

            @pl.when(mine)
            def _():
                keep(zq, s).wait()

            @pl.when(jnp.logical_not(mine))
            def _():
                give(zq, s).wait_send()

    for far in (0, 1, 2, 3):

        @pl.when((z != far) | (core != kept))
        def _():
            remote(
                parts.at[far], parts.at[far], osend.at[0], orecv.at[far], at(z, x, 1 - core)
            ).wait_recv()

    fetch.wait()

    def total(i, carry):
        block = pl.ds(pl.multiple_of(i * 16, 16), 16)
        value = hid_ref[block, :].astype(jnp.float32)
        mixed = parts[0, block, :].astype(jnp.float32)
        for far in (1, 2, 3):
            mixed += parts[far, block, :].astype(jnp.float32)
        target_ref[block, :] = (value + mixed).astype(jnp.bfloat16)
        return carry

    lax.fori_loop(0, ROWS // 16, total, 0)


def attend(length, qkv, w_out, hidden):
    vmem = pl.BlockSpec(memory_space=pltpu.VMEM)
    return pl.pallas_call(
        attend_kernel,
        name="attend",
        out_shape=jax.ShapeDtypeStruct((ROWS, HW), jnp.bfloat16),
        in_specs=[
            pl.BlockSpec(memory_space=pltpu.SMEM),
            vmem,
            vmem,
            pl.BlockSpec(memory_space=pltpu.HBM),
        ],
        out_specs=vmem,
        scratch_shapes=[
            pltpu.VMEM((ROWS, HW), jnp.bfloat16),
            pltpu.VMEM((4, 2, 256, 256), jnp.bfloat16),
            pltpu.VMEM((2, 2, 256, 256), jnp.bfloat16),
            pltpu.VMEM((2, 256, HW), jnp.bfloat16),
            pltpu.VMEM((4, ROWS, HW), jnp.bfloat16),
            pltpu.SemaphoreType.DMA((2,)),
            pltpu.SemaphoreType.DMA((2,)),
            pltpu.SemaphoreType.DMA((4,)),
            pltpu.SemaphoreType.DMA((4,)),
            pltpu.SemaphoreType.DMA,
        ],
        compiler_params=pltpu.CompilerParams(
            collective_id=1, has_side_effects=True, vmem_limit_bytes=48 * MIB
        ),
    )(length, qkv, w_out, hidden)


def rms_norm(rows, gain):
    return rows * lax.rsqrt(jnp.mean(rows * rows, axis=-1, keepdims=True) + 1e-06) * gain


def valid_rows(first_row, count, group_lengths):
    rows = first_row + jnp.arange(count, dtype=jnp.int32)
    caption = rows // LEN
    position = rows % LEN
    picked = jnp.where(
        caption[:, None] == jnp.arange(SEQS, dtype=jnp.int32)[None, :], group_lengths[None, :], 0
    )
    return position < jnp.sum(picked, axis=1)


def shards(
    hidden_in, norm_gain, w_qkv, w_out, lengths, student_in, student_gain, proj_weight, loss_scale
):
    rows_dev = hidden_in.shape[0]
    tp_place = lax.axis_index("tp")
    group = lax.axis_index("dp")
    group_lengths = lax.dynamic_slice_in_dim(lengths, group * SEQS, SEQS)
    count = jnp.sum(lengths).astype(jnp.float32)
    factor = 2.0 * loss_scale[0] / (count * HW)
    own_rows = student_in.astype(jnp.float32)

    qkv, w_out_all = project(hidden_in, norm_gain.reshape(1, D), w_qkv, w_out)
    length = lax.dynamic_slice_in_dim(lengths, group * SEQS + tp_place % 2, 1)
    target = attend(length, qkv, w_out_all, hidden_in)

    proj_whole = lax.all_gather(proj_weight, "tp", axis=0, tiled=True)
    student_norm = rms_norm(own_rows, student_gain).astype(jnp.bfloat16)
    mapped = lax.dot_general(
        student_norm, proj_whole, (((1,), (1,)), ((), ())), preferred_element_type=jnp.float32
    )
    valid = valid_rows(tp_place * rows_dev, rows_dev, group_lengths)
    diff = jnp.where(valid[:, None], mapped - target.astype(jnp.float32), 0.0)
    loss_part = jnp.sum(diff * diff)
    delta = (diff * factor).astype(jnp.bfloat16)
    norm_back = jnp.dot(delta, proj_whole, preferred_element_type=jnp.float32)
    proj_part = lax.psum_scatter(
        lax.dot_general(
            delta, student_norm, (((0,), (0,)), ((), ())), preferred_element_type=jnp.float32
        ).astype(jnp.bfloat16),
        "tp",
        scatter_dimension=0,
        tiled=True,
    )
    proj_total = lax.psum(proj_part, "dp").astype(jnp.float32)
    unused, pull_back = jax.vjp(rms_norm, own_rows, student_gain)
    row_grad, gain_part = pull_back(norm_back)
    loss_total, gain_total = lax.psum((loss_part, gain_part), ("tp", "dp"))
    return (
        row_grad.astype(jnp.bfloat16),
        proj_total.astype(jnp.bfloat16),
        gain_total,
        loss_total / (count * HW),
    )


def solution(mesh):
    placed = (
        P(("dp", "tp"), None),
        P(),
        P(None, None, "tp"),
        P("tp", None),
        P(),
        P(("dp", "tp"), None),
        P(),
        P("tp", None),
        P(),
    )
    return jax.shard_map(
        shards,
        mesh=mesh,
        in_specs=placed,
        out_specs=(P(("dp", "tp"), None), P("tp", None), P(), P()),
        check_vma=False,
    )
```

time: 611 us -> 438 us (0.72)
  waiting for transfers between devices: 410 us -> 97.4 us
  Pallas kernels: 0 us -> 224 us
  matrix products: 78.3 us -> 15.9 us
  local copies, waits for them, and re-layouts: 23.7 us -> 5.67 us
  other arithmetic: 9.81 us -> 2.42 us
    pallas_call x0 -> x2, Pallas kernels: none -> 224 us  [the longest x1 152 us: project(): pl.pallas_call(project_kernel, name='project', out_shape=(jax.ShapeDtypeS...]
    reduce_scatter x2 -> x1, waiting for transfers between devices: 173 us -> 14.6 us  [shards(): lax.psum_scatter(lax.dot_general(delta, student_norm, (((0,), (0,)), ((),...]
    all_gather x1 -> x0, waiting for transfers between devices: 154 us -> none  [shards(): lax.all_gather(normed_local, 'tp', axis=0, tiled=True)]
    dot_general x5 -> x1, matrix products: 51.4 us -> 5.19 us  [shards(): lax.dot_general(delta, student_norm, (((0,), (0,)), ((), ())), preferred_...]
    sub x2 -> x0, matrix products: 15.1 us -> none  [single_caption(): weights = jnp.exp(scores - jnp.max(scores, axis=-1, keepdims=True))]
    dynamic_slice x8 -> x1, local copies, waits for them, and re-layouts: 10.2 us -> 1.24 us  [shards(): length = lax.dynamic_slice_in_dim(lengths, group * SEQS + tp_place % 2, 1)]
  transfers between devices with their start and end apart: 5 -> 3, of which waited for: 4 -> 2; matrix products, arithmetic and copies ran while one was open for 15% -> 2% of each run, Pallas kernels for 0% -> 52%
where the time goes in v1:
time: 438 us; the launch traced here: 433 us
  Pallas kernels  224 us (51%)
  waiting for transfers between devices  97.4 us (22%)
  blocking collectives  69.8 us (16%)
  between operations  17 us (4%)
  matrix products  15.9 us (4%)
  local copies, waits for them, and re-layouts  5.67 us (1%)
    pallas_call x1, Pallas kernels, project(): pl.pallas_call(project_kernel, name='project', out_shape=(jax.ShapeDtypeS...  152 us
    psum x1, waiting for transfers between devices, shards(): proj_total = lax.psum(proj_part, 'dp').astype(jnp.float32)  82.1 us
    pallas_call x1, Pallas kernels, attend(): pl.pallas_call(attend_kernel, name='attend', out_shape=jax.ShapeDtypeStru...  72.9 us
    psum x1, blocking collectives, shards(): loss_total, gain_total = lax.psum((loss_part, gain_part), ('tp', 'dp'))  69.8 us
    reduce_scatter x1, waiting for transfers between devices, shards(): lax.psum_scatter(lax.dot_general(delta, student_norm, (((0,), (0,)), ((),...  14.6 us
  transfers between devices with their start and end apart: 3, of which 2 were waited for; matrix products, arithmetic and copies ran while one was open for 2% of the time, Pallas kernels for 52%

profile of v1, /device:TPU:1, one launch (start us, length us, event | category | flops | bytes accessed | tf_op | source)
XLA Modules:
  0.0 432.7 jit_solution(1062780508513875273)
XLA Ops:
  7.2 0.0 all-gather.2.cloned.1.call-start
  7.2 0.7 all-gather.2.cloned.1.call-update
  7.9 0.0 reduce-scatter.2.cloned.1.call-start
  8.0 1.3 reduce_sum.56
  9.3 1.2 dynamic_slice.7.len_ref
  10.5 0.7 dynamic_slice.6
  12.6 0.0 copy-start
  12.6 151.6 %project.1 = (bf16[6,1024,256]{2,1,0:T(8,128)(2,1)}, bf16[4,256,3584]{2,1,0:T(8,128)(2,1)}) custom-call(bf16[128,7168]{1,0:T(8,128)(2,1)} %hid_hbm.1, f32[1,7168]{1,0:T(1,128)} %bitcast.4, bf16[3,7168,256]{2,1,0:T(8,128)(2,1)} %w_hbm.1, bf16[256,3584]{1,0:T(8,128)(2,1)} %wout_hbm.1), custom_call_target="tpu_custom_call" | custom-call | tf_op jit(solution)/shard_map/project/pallas_call | solution.py:262
  164.2 1.9 copy-done.1
  166.1 72.9 %attend.1 = bf16[128,3584]{1,0:T(8,128)(2,1)S(1)} custom-call(s32[1]{0:T(128)} %dynamic_slice.7.len_ref, bf16[6,1024,256]{2,1,0:T(8,128)(2,1)S(1)} %copy-done.1, bf16[4,256,3584]{2,1,0:T(8,128)(2,1)} %get-tuple-element.7.wout_ref, bf16[128,7168]{1,0:T(8,128)(2,1)S(1)} %copy-done), custom_call_target="tpu_custom_call" | custom-call | tf_op jit(solution)/shard_map/attend/pallas_call | solution.py:416
  239.0 0.1 fusion.11
  239.1 0.1 fusion.6
  239.2 0.0 all-gather.2.cloned.1.call-done
  239.3 6.3 %multiply_reduce_fusion = (f32[]{:T(128)}, f32[128,3584]{1,0:T(8,128)S(1)}) fusion(bf16[128,3584]{1,0:T(8,128)(2,1)S(1)} %attend.1, bf16[3584,1024]{1,0:T(8,128)(2,1)} %all-gather.2.cloned.1.call-done, bf16[128,1024]{1,0:T(8,128)(2,1)S(1)} %copy-done.2, f32[1024]{0:T(1024)S(1)} %copy-done.3, f32[128]{0:T(128)S(1)} %fusion.13, pred[128]{0:T(512)(128)(4,1)S(1)} %fusion.12), kind=kOutput, calls=%fused_computation.3 | convolution fusion | flops 942342144 | bytes 10359428 | tf_op jit(solution)/shard_map/dot_general | solution.py:476
  245.6 5.2 %convolution_convert_fusion = bf16[3584,1024]{1,0:T(8,128)(2,1)} fusion(f32[128,3584]{1,0:T(8,128)S(1)} %get-tuple-element.14, f32[]{:T(128)S(6)} %div.36, bf16[128,1024]{1,0:T(8,128)(2,1)S(1)} %copy-done.2, f32[1024]{0:T(1024)S(1)} %copy-done.3, f32[128]{0:T(128)S(1)} %fusion.13), kind=kOutput, calls=%fused_computation | convolution fusion | flops 944635904 | bytes 9441796 | tf_op jit(solution)/shard_map/dot_general | solution.py:485
  250.8 0.0 reduce-scatter.2.cloned.1.call-update
  250.8 0.0 all-reduce.3.cloned.1.call-start
  250.8 4.4 %fusion.4 = (f32[1024]{0:T(1024)S(1)}, f32[128]{0:T(128)S(1)}, f32[128,1024]{1,0:T(8,128)S(1)}) fusion(bf16[128,1024]{1,0:T(8,128)(2,1)S(1)} %copy-done.2, f32[128]{0:T(128)S(1)} %fusion.13, f32[1024]{0:T(1024)S(1)} %copy-done.3, bf16[3584,1024]{1,0:T(8,128)(2,1)} %all-gather.2.cloned.1.call-done, f32[128,3584]{1,0:T(8,128)S(1)} %get-tuple-element.14, ...), kind=kOutput, calls=%fused_computation.13 | convolution fusion | flops 941357952 | bytes 9970692 | tf_op jit(solution)/shard_map/dot_general | solution.py:483
  255.2 69.8 %all-reduce = (f32[1024]{0:T(1024)}, f32[]{:T(128)}) all-reduce(f32[1024]{0:T(1024)S(1)} %get-tuple-element.8, f32[]{:T(128)} %get-tuple-element.13), channel_id=1, replica_groups=mesh['tp'=16,'dp'=8] {'tp','dp'}, use_global_device_ids=true, to_apply=%region_7.8 | all-reduce | flops 1025 | bytes 8200 | tf_op jit(solution)/shard_map/psum | solution.py:495
  325.6 14.6 %reduce-scatter.2.cloned.1.call-done = bf16[224,1024]{1,0:T(8,128)(2,1)} async-done(((bf16[3584,1024]{1,0:T(8,128)(2,1)}), bf16[224,1024]{1,0:T(8,128)(2,1)}) %reduce-scatter.2.cloned.1.call-update) | async-done | bytes 458768 | tf_op jit(solution)/shard_map/reduce_scatter | solution.py:484
  340.2 0.0 all-reduce.3.cloned.1.call-update
  340.3 0.9 fusion.5
  341.1 82.1 %all-reduce.3.cloned.1.call-done = bf16[224,1024]{1,0:T(8,128)(2,1)} async-done(((bf16[224,1024]{1,0:T(8,128)(2,1)}), bf16[224,1024]{1,0:T(8,128)(2,1)}) %all-reduce.3.cloned.1.call-update) | async-done | bytes 458768 | tf_op jit(solution)/shard_map/psum | solution.py:492
  423.3 1.8 copy.15
  (10 shorter events, 0.1 us)
Async XLA Ops:
  7.2 232.1 %all-gather.2.cloned.1.call-start = ((), (), s32[]{:S(2)}) async-start(), calls=%async_computation.1 | async-start | bytes 7798784 | tf_op jit(solution)/shard_map/all_gather | solution.py:474
  7.9 332.3 %reduce-scatter.2.cloned.1.call-start = ((), (), s32[]{:S(2)}) async-start(), calls=%async_computation.2 | async-start | bytes 7798784 | tf_op jit(solution)/shard_map/reduce_scatter | solution.py:484
  12.6 151.7 %copy-start = (bf16[128,7168]{1,0:T(8,128)(2,1)S(1)}, bf16[128,7168]{1,0:T(8,128)(2,1)}, u32[]{:S(2)}) copy-start(bf16[128,7168]{1,0:T(8,128)(2,1)} %hid_hbm.1) | copy-start | bytes 5505028
  164.2 1.9 copy-start.1
  166.1 73.0 %copy-start.2 = (bf16[128,1024]{1,0:T(8,128)(2,1)S(1)}, bf16[128,1024]{1,0:T(8,128)(2,1)}, u32[]{:S(2)}) copy-start(bf16[128,1024]{1,0:T(8,128)(2,1)} %param.14) | copy-start | bytes 786436
  166.1 73.2 %copy-start.3 = (f32[1024]{0:T(1024)S(1)}, f32[1024]{0:T(1024)}, u32[]{:S(2)}) copy-start(f32[1024]{0:T(1024)} %param.15) | copy-start | bytes 12292
  250.8 172.5 %all-reduce.3.cloned.1.call-start = ((), (), s32[]{:S(2)}) async-start(), calls=%async_computation.3 | async-start | bytes 917504 | tf_op jit(solution)/shard_map/psum | solution.py:492
Sparse Core Ops, SparseCore 0:
  9.7 85.3 all-gather.1
  250.9 89.2 reduce-scatter.1
  342.7 80.5 all-reduce.2

commit v2 on v1

--- a/solution.py
+++ b/solution.py
@@ -13,6 +13,8 @@
 LEN = 1024
 SEQS = 2
 D = 7168
+DS = 1024
+PROJ = 224
 ROWS = 128
 FIRST = 80
 MESH = pl.DeviceIdType.MESH
@@ -33,10 +35,19 @@
     return {"tp": z * 4 + (1 - x) * 2 + core, "dp": (1 - dp // 4) * 4 + dp % 4}
 
 
+def beside(z, x, core, i):
+    dp = lax.axis_index("dp")
+    return {"tp": z * 4 + x * 2 + core, "dp": dp // 4 * 4 + (dp + i) % 4}
+
+
 def remote(src, dst, send, recv, device):
     return pltpu.make_async_remote_copy(
         src_ref=src, dst_ref=dst, send_sem=send, recv_sem=recv, device_id=device, device_id_type=MESH
     )
+
+
+def rms_norm(rows, gain):
+    return rows * lax.rsqrt(jnp.mean(rows * rows, axis=-1, keepdims=True) + 1e-06) * gain
 
 
 def greet(devices):
@@ -290,20 +301,98 @@
 
 
 def attend_kernel(
-    len_ref, qkv_ref, wout_ref, hid_hbm, target_ref, hid_ref, ctx, ctx_in, stage, parts, send, recv, osend, orecv, local
+    len_ref,
+    qkv_ref,
+    wout_ref,
+    hid_hbm,
+    proj_ref,
+    student_ref,
+    sgain_ref,
+    target_ref,
+    proj_all,
+    norm_all,
+    hid_ref,
+    ctx,
+    ctx_in,
+    stage,
+    parts,
+    norm_own,
+    send,
+    recv,
+    osend,
+    orecv,
+    psend,
+    precv,
+    nsend,
+    nrecv,
+    ysend,
+    yrecv,
+    csend,
+    crecv,
+    local,
 ):
     z, x, core = place()
     other = 1 - x
     kept = z // 2
     length = len_ref[0]
-    fetch = pltpu.make_async_copy(hid_hbm.at[:, pl.ds(0, HW)], hid_ref, local)
+    fetch = pltpu.make_async_copy(hid_hbm.at[:, pl.ds(0, HW)], hid_ref, local.at[0])
     fetch.start()
-
+    rows = student_ref[...].astype(jnp.float32)
+    norm_own[...] = rms_norm(rows, sgain_ref[...]).astype(jnp.bfloat16)
+
+    peers = [(z + i, xx) for i in range(4) for xx in (x, other)][1:]
     greet(
         [at(z, x, 1 - core)]
-        + [at(zz, x, c) for zz in (z + 1, z + 2, z + 3) for c in (0, 1)]
-        + [at(z, other, core)]
+        + [at(zz, xx, c) for zz, xx in peers for c in (0, 1)]
+        + [beside(z, x, core, i) for i in (1, 2, 3)]
     )
+
+    y = lax.axis_index("dp") % 4
+    chip = z * 2 + x
+    quarter = proj_ref.at[:, pl.ds(pl.multiple_of(y * 256, 256), 256)]
+    proj_here = pltpu.make_async_copy(quarter, proj_all.at[y, chip, core], local.at[1])
+    norm_here = pltpu.make_async_copy(norm_own, norm_all.at[core, chip], local.at[2])
+    proj_going = [
+        remote(quarter, proj_all.at[y, chip, core], psend.at[i], precv.at[chip], at(zz, xx, core))
+        for i, (zz, xx) in enumerate(peers)
+    ]
+    norm_going = [
+        remote(norm_own, norm_all.at[core, chip], nsend.at[i], nrecv.at[chip], at(zz, xx, core))
+        for i, (zz, xx) in enumerate(peers)
+    ]
+    for copy in [proj_here, norm_here] + proj_going + norm_going:
+        copy.start()
+
+    def along(i):
+        ref = proj_all.at[y, :, core]
+        return remote(ref, ref, ysend.at[i - 1], yrecv.at[y], beside(z, x, core, i))
+
+    def spread():
+        proj_here.wait()
+        for zz, xx in peers:
+            ref = proj_all.at[y, (zz % 4) * 2 + xx, core]
+            remote(ref, ref, psend.at[0], precv.at[(zz % 4) * 2 + xx], at(z, x, 1 - core)).wait_recv()
+        for i in (1, 2, 3):
+            along(i).start()
+
+    def sibling(c):
+        return [
+            remote(norm_all.at[c], norm_all.at[c], csend.at[0], crecv.at[0], at(z, x, 1 - core)),
+            remote(proj_all.at[:, :, c], proj_all.at[:, :, c], csend.at[1], crecv.at[1], at(z, x, 1 - core)),
+        ]
+
+    def share_norm():
+        norm_here.wait()
+        for zz, xx in peers:
+            ref = norm_all.at[core, (zz % 4) * 2 + xx]
+            remote(ref, ref, nsend.at[0], nrecv.at[(zz % 4) * 2 + xx], at(z, x, 1 - core)).wait_recv()
+        sibling(core)[0].start()
+
+    def share_proj():
+        for i in (1, 2, 3):
+            ref = proj_all.at[(y + i) % 4, :, core]
+            remote(ref, ref, ysend.at[0], yrecv.at[(y + i) % 4], at(z, x, 1 - core)).wait_recv()
+        sibling(core)[1].start()
 
     def attend(chunk, keys, zq, mine):
         start = pl.multiple_of(chunk * 256, 256)
@@ -348,6 +437,7 @@
         keys = (zq + 1) * 512
         attend(zq * 2 + other, keys, zq, 0)
         swap(zq).start()
+        (spread, share_norm)[zq]()
         attend(zq * 2 + x, keys, zq, 1)
         swap(zq).wait_recv()
 
@@ -376,6 +466,7 @@
             def _():
                 give(zq, s).start()
 
+    share_proj()
     for zq in (0, 1):
         swap(zq).wait_send()
         for s in (0, 1):
@@ -397,6 +488,10 @@
                 parts.at[far], parts.at[far], osend.at[0], orecv.at[far], at(z, x, 1 - core)
             ).wait_recv()
 
+    for copy in proj_going + norm_going + [along(i) for i in (1, 2, 3)] + sibling(core):
+        copy.wait_send()
+    for copy in sibling(1 - core):
+        copy.wait_recv()
     fetch.wait()
 
     def total(i, carry):
@@ -411,94 +506,278 @@
     lax.fori_loop(0, ROWS // 16, total, 0)
 
 
-def attend(length, qkv, w_out, hidden):
+def attend(length, qkv, w_out, hidden, proj, student, gain):
     vmem = pl.BlockSpec(memory_space=pltpu.VMEM)
+    hbm = pl.BlockSpec(memory_space=pltpu.HBM)
     return pl.pallas_call(
         attend_kernel,
         name="attend",
-        out_shape=jax.ShapeDtypeStruct((ROWS, HW), jnp.bfloat16),
-        in_specs=[
-            pl.BlockSpec(memory_space=pltpu.SMEM),
-            vmem,
-            vmem,
-            pl.BlockSpec(memory_space=pltpu.HBM),
-        ],
-        out_specs=vmem,
+        out_shape=(
+            jax.ShapeDtypeStruct((ROWS, HW), jnp.bfloat16),
+            jax.ShapeDtypeStruct((4, 8, 2, PROJ, 256), jnp.bfloat16),
+            jax.ShapeDtypeStruct((2, 8, ROWS, DS), jnp.bfloat16),
+        ),
+        in_specs=[pl.BlockSpec(memory_space=pltpu.SMEM), vmem, vmem, hbm, vmem, vmem, vmem],
+        out_specs=(vmem, hbm, hbm),
         scratch_shapes=[
             pltpu.VMEM((ROWS, HW), jnp.bfloat16),
             pltpu.VMEM((4, 2, 256, 256), jnp.bfloat16),
             pltpu.VMEM((2, 2, 256, 256), jnp.bfloat16),
             pltpu.VMEM((2, 256, HW), jnp.bfloat16),
             pltpu.VMEM((4, ROWS, HW), jnp.bfloat16),
-            pltpu.SemaphoreType.DMA((2,)),
-            pltpu.SemaphoreType.DMA((2,)),
-            pltpu.SemaphoreType.DMA((4,)),
-            pltpu.SemaphoreType.DMA((4,)),
-            pltpu.SemaphoreType.DMA,
-        ],
+            pltpu.VMEM((ROWS, DS), jnp.bfloat16),
+        ]
+        + [pltpu.SemaphoreType.DMA((n,)) for n in (2, 2, 4, 4, 7, 8, 7, 8, 3, 4, 2, 2, 3)],
         compiler_params=pltpu.CompilerParams(
             collective_id=1, has_side_effects=True, vmem_limit_bytes=48 * MIB
         ),
-    )(length, qkv, w_out, hidden)
-
-
-def rms_norm(rows, gain):
-    return rows * lax.rsqrt(jnp.mean(rows * rows, axis=-1, keepdims=True) + 1e-06) * gain
-
-
-def valid_rows(first_row, count, group_lengths):
-    rows = first_row + jnp.arange(count, dtype=jnp.int32)
-    caption = rows // LEN
-    position = rows % LEN
-    picked = jnp.where(
-        caption[:, None] == jnp.arange(SEQS, dtype=jnp.int32)[None, :], group_lengths[None, :], 0
+    )(length, qkv, w_out, hidden, proj, student, gain)
+
+
+def student_kernel(
+    len_ref,
+    factor_ref,
+    target_ref,
+    student_ref,
+    gain_ref,
+    proj_ref,
+    norm_ref,
+    grad_ref,
+    out_ref,
+    stat_ref,
+    delta,
+    flipped,
+    flipped_in,
+    stat,
+    stat_in,
+    total,
+    total_in,
+    piece,
+    piece_in,
+    summed,
+    dsend,
+    drecv,
+    ssend,
+    srecv,
+    tsend,
+    trecv,
+    gsend,
+    grecv,
+    asend,
+    arecv,
+    local,
+):
+    z, x, core = place()
+    tp = lax.axis_index("tp")
+    dp = lax.axis_index("dp")
+    length = len_ref[0]
+    factor = factor_ref[0]
+    lane = (core * 8 + z * 2 + x) * ROWS
+
+    def mate(i):
+        return (tp + i) % 16
+
+    def group(i):
+        return (dp + i) % 8
+
+    greet([{"tp": mate(i)} for i in range(1, 16)] + [{"dp": group(i)} for i in range(1, 8)])
+
+    rows = student_ref[...].astype(jnp.float32)
+    scale = lax.rsqrt(jnp.mean(rows * rows, axis=-1, keepdims=True) + 1e-06)
+    normed = (rows * scale * gain_ref[...]).astype(jnp.bfloat16)
+    position = (tp % 8) * ROWS + lax.broadcasted_iota(jnp.int32, (ROWS, 1), 0)
+    valid = position < length
+
+    def compare(n, loss):
+        base = pl.multiple_of(n * 512, 512)
+        mapped = jnp.zeros((ROWS, 512), jnp.float32)
+        for k in range(4):
+            mapped += lax.dot_general(
+                normed[:, k * 256 : (k + 1) * 256],
+                proj_ref[k, pl.ds(base, 512), :],
+                (((1,), (1,)), ((), ())),
+                preferred_element_type=jnp.float32,
+            )
+        diff = jnp.where(valid, mapped - target_ref[:, pl.ds(base, 512)].astype(jnp.float32), 0.0)
+        scaled = diff * factor
+        delta[:, pl.ds(base, 512)] = scaled.astype(jnp.bfloat16)
+        for t in range(4):
+            tile = scaled[:, t * 128 : (t + 1) * 128]
+            flipped[pl.ds(pl.multiple_of(base + t * 128, 128), 128), :] = tile.T.astype(jnp.bfloat16)
+        return loss + jnp.sum(diff * diff)
+
+    loss = lax.fori_loop(0, HW // 512, compare, jnp.float32(0.0))
+
+    def flip(i):
+        src = flipped.at[pl.ds(pl.multiple_of(mate(i) * PROJ, 16), PROJ)]
+        dst = flipped_in.at[:, pl.ds(pl.multiple_of(lane, 128), ROWS)]
+        return remote(src, dst, dsend.at[i - 1], drecv.at[tp], {"tp": mate(i)})
+
+    own_flip = pltpu.make_async_copy(
+        flipped.at[pl.ds(pl.multiple_of(tp * PROJ, 16), PROJ)],
+        flipped_in.at[:, pl.ds(pl.multiple_of(lane, 128), ROWS)],
+        local.at[0],
     )
-    return position < jnp.sum(picked, axis=1)
+    for i in range(1, 16):
+        flip(i).start()
+    own_flip.start()
+
+    back = [
+        jnp.dot(delta[...], proj_ref[k], preferred_element_type=jnp.float32) for k in range(4)
+    ]
+    dots = jnp.zeros((ROWS, 1), jnp.float32)
+    for k in range(4):
+        cols = slice(k * 256, (k + 1) * 256)
+        dots += jnp.sum(back[k] * gain_ref[:, cols] * rows[:, cols], axis=-1, keepdims=True)
+    shift = dots * (scale * scale * scale) * (1.0 / DS)
+    for k in range(4):
+        cols = slice(k * 256, (k + 1) * 256)
+        grad_ref[:, cols] = (
+            back[k] * gain_ref[:, cols] * scale - rows[:, cols] * shift
+        ).astype(jnp.bfloat16)
+        part = jnp.sum(back[k] * (rows[:, cols] * scale), axis=0, keepdims=True)
+        stat[2 * k : 2 * k + 1, :] = part[:, :128]
+        stat[2 * k + 1 : 2 * k + 2, :] = part[:, 128:]
+    stat[8:16, :] = jnp.zeros((8, 128), jnp.float32) + loss
+
+    def tell(i):
+        return remote(stat, stat_in.at[tp], ssend.at[i - 1], srecv.at[tp], {"tp": mate(i)})
+
+    for i in range(1, 16):
+        tell(i).start()
+
+    for i in range(1, 16):
+        far = mate(i)
+        got = flipped_in.at[
+            :, pl.ds(pl.multiple_of(((far % 2) * 8 + far // 2) * ROWS, 128), ROWS)
+        ]
+        remote(got, got, dsend.at[0], drecv.at[far], {"tp": far}).wait_recv()
+    own_flip.wait()
+
+    def hand(i):
+        return remote(piece.at[group(i)], piece_in.at[dp], gsend.at[i - 1], grecv.at[dp], {"dp": group(i)})
+
+    for k in range(4):
+        out = jnp.dot(
+            flipped_in[...], norm_ref[:, k * 256 : (k + 1) * 256], preferred_element_type=jnp.float32
+        ).astype(jnp.bfloat16)
+        piece[2 * k] = out[:, :128]
+        piece[2 * k + 1] = out[:, 128:]
+    for i in range(1, 8):
+        hand(i).start()
+
+    for i in range(1, 16):
+        far = stat_in.at[mate(i)]
+        remote(far, far, ssend.at[0], srecv.at[mate(i)], {"tp": mate(i)}).wait_recv()
+    stat_in[tp] = stat[...]
+    total[...] = jnp.sum(stat_in[...], axis=0)
+
+    def tell_groups(i):
+        return remote(total, total_in.at[dp], tsend.at[i - 1], trecv.at[dp], {"dp": group(i)})
+
+    for i in range(1, 8):
+        tell_groups(i).start()
+
+    for i in range(1, 8):
+        far = piece_in.at[group(i)]
+        remote(far, far, gsend.at[0], grecv.at[group(i)], {"dp": group(i)}).wait_recv()
+    piece_in[dp] = piece[dp]
+    acc = jnp.zeros((PROJ, 128), jnp.float32)
+    for k in range(8):
+        acc += piece_in[k].astype(jnp.float32)
+    summed[...] = acc.astype(jnp.bfloat16)
+
+    def column(g):
+        return out_ref.at[:, pl.ds(pl.multiple_of(g * 128, 128), 128)]
+
+    def publish(i):
+        return remote(summed, column(dp), asend.at[i - 1], arecv.at[dp], {"dp": group(i)})
+
+    own_column = pltpu.make_async_copy(summed, column(dp), local.at[1])
+    own_column.start()
+    for i in range(1, 8):
+        publish(i).start()
+
+    for i in range(1, 8):
+        far = total_in.at[group(i)]
+        remote(far, far, tsend.at[0], trecv.at[group(i)], {"dp": group(i)}).wait_recv()
+    total_in[dp] = total[...]
+    stat_ref[...] = jnp.sum(total_in[...], axis=0)
+
+    for i in range(1, 8):
+        far = column(group(i))
+        remote(far, far, asend.at[0], arecv.at[group(i)], {"dp": group(i)}).wait_recv()
+    own_column.wait()
+    for i in range(1, 16):
+        flip(i).wait_send()
+        tell(i).wait_send()
+    for i in range(1, 8):
+        hand(i).wait_send()
+        tell_groups(i).wait_send()
+        publish(i).wait_send()
+
+
+def student(length, factor, target, rows, gain, proj, norm):
+    vmem = pl.BlockSpec(memory_space=pltpu.VMEM)
+    smem = pl.BlockSpec(memory_space=pltpu.SMEM)
+    return pl.pallas_call(
+        student_kernel,
+        name="student",
+        out_shape=(
+            jax.ShapeDtypeStruct((ROWS, DS), jnp.bfloat16),
+            jax.ShapeDtypeStruct((PROJ, DS), jnp.bfloat16),
+            jax.ShapeDtypeStruct((16, 128), jnp.float32),
+        ),
+        in_specs=[smem, smem] + [vmem] * 5,
+        out_specs=(vmem, vmem, vmem),
+        scratch_shapes=[
+            pltpu.VMEM((ROWS, HW), jnp.bfloat16),
+            pltpu.VMEM((HW, ROWS), jnp.bfloat16),
+            pltpu.VMEM((PROJ, 2 * LEN), jnp.bfloat16),
+            pltpu.VMEM((16, 128), jnp.float32),
+            pltpu.VMEM((16, 16, 128), jnp.float32),
+            pltpu.VMEM((16, 128), jnp.float32),
+            pltpu.VMEM((8, 16, 128), jnp.float32),
+            pltpu.VMEM((8, PROJ, 128), jnp.bfloat16),
+            pltpu.VMEM((8, PROJ, 128), jnp.bfloat16),
+            pltpu.VMEM((PROJ, 128), jnp.bfloat16),
+        ]
+        + [pltpu.SemaphoreType.DMA((n,)) for n in (15, 16, 15, 16, 7, 8, 7, 8, 7, 8, 2)],
+        compiler_params=pltpu.CompilerParams(
+            collective_id=2, has_side_effects=True, vmem_limit_bytes=48 * MIB
+        ),
+    )(length, factor, target, rows, gain, proj, norm)
 
 
 def shards(
     hidden_in, norm_gain, w_qkv, w_out, lengths, student_in, student_gain, proj_weight, loss_scale
 ):
-    rows_dev = hidden_in.shape[0]
-    tp_place = lax.axis_index("tp")
+    tp = lax.axis_index("tp")
     group = lax.axis_index("dp")
-    group_lengths = lax.dynamic_slice_in_dim(lengths, group * SEQS, SEQS)
     count = jnp.sum(lengths).astype(jnp.float32)
-    factor = 2.0 * loss_scale[0] / (count * HW)
-    own_rows = student_in.astype(jnp.float32)
+    factor = 2.0 * loss_scale / (count * HW)
+    gain = student_gain.reshape(1, DS)
 
     qkv, w_out_all = project(hidden_in, norm_gain.reshape(1, D), w_qkv, w_out)
-    length = lax.dynamic_slice_in_dim(lengths, group * SEQS + tp_place % 2, 1)
-    target = attend(length, qkv, w_out_all, hidden_in)
-
-    proj_whole = lax.all_gather(proj_weight, "tp", axis=0, tiled=True)
-    student_norm = rms_norm(own_rows, student_gain).astype(jnp.bfloat16)
-    mapped = lax.dot_general(
-        student_norm, proj_whole, (((1,), (1,)), ((), ())), preferred_element_type=jnp.float32
+    target, proj_all, norm_all = attend(
+        lax.dynamic_slice_in_dim(lengths, group * SEQS + tp % 2, 1),
+        qkv,
+        w_out_all,
+        hidden_in,
+        proj_weight,
+        student_in,
+        gain,
     )
-    valid = valid_rows(tp_place * rows_dev, rows_dev, group_lengths)
-    diff = jnp.where(valid[:, None], mapped - target.astype(jnp.float32), 0.0)
-    loss_part = jnp.sum(diff * diff)
-    delta = (diff * factor).astype(jnp.bfloat16)
-    norm_back = jnp.dot(delta, proj_whole, preferred_element_type=jnp.float32)
-    proj_part = lax.psum_scatter(
-        lax.dot_general(
-            delta, student_norm, (((0,), (0,)), ((), ())), preferred_element_type=jnp.float32
-        ).astype(jnp.bfloat16),
-        "tp",
-        scatter_dimension=0,
-        tiled=True,
+    row_grad, proj_grad, stat = student(
+        lax.dynamic_slice_in_dim(lengths, group * SEQS + tp // 8, 1),
+        factor,
+        target,
+        student_in,
+        gain,
+        proj_all.reshape(4, HW, 256),
+        norm_all.reshape(2 * LEN, DS),
     )
-    proj_total = lax.psum(proj_part, "dp").astype(jnp.float32)
-    unused, pull_back = jax.vjp(rms_norm, own_rows, student_gain)
-    row_grad, gain_part = pull_back(norm_back)
-    loss_total, gain_total = lax.psum((loss_part, gain_part), ("tp", "dp"))
-    return (
-        row_grad.astype(jnp.bfloat16),
-        proj_total.astype(jnp.bfloat16),
-        gain_total,
-        loss_total / (count * HW),
-    )
+    return row_grad, proj_grad, stat[:8].reshape(DS), stat[8, 0] / (count * HW)
 
 
 def solution(mesh):

time: 438 us -> 279 us (0.64); the launches traced: 433 us -> 278 us
  waiting for transfers between devices: 97.4 us -> 0 us
  blocking collectives: 69.8 us -> 0 us
  Pallas kernels: 224 us -> 268 us
  matrix products: 15.9 us -> 0 us
  between operations: 17 us -> 3.89 us
    psum x1 -> x0, waiting for transfers between devices: 82.1 us -> none  [shards(): proj_total = lax.psum(proj_part, 'dp').astype(jnp.float32)]
    pallas_call x1 -> x2, Pallas kernels: 72.9 us -> 150 us  [the longest x1 105 us: attend(): pl.pallas_call(attend_kernel, name='attend', out_shape=(jax.ShapeDtypeStr...]
    psum x1 -> x0, blocking collectives: 69.8 us -> none  [shards(): loss_total, gain_total = lax.psum((loss_part, gain_part), ('tp', 'dp'))]
    pallas_call x1, Pallas kernels: 152 us -> 117 us  [project(): pl.pallas_call(project_kernel, name='project', out_shape=(jax.ShapeDtypeS...]
    dot_general x3 -> x0, matrix products: 15.9 us -> none  [the longest x1 6.3 us: shards(): lax.dot_general(student_norm, proj_whole, (((1,), (1,)), ((), ())), prefe...]
    reduce_scatter x1 -> x0, waiting for transfers between devices: 14.6 us -> none  [shards(): lax.psum_scatter(lax.dot_general(delta, student_norm, (((0,), (0,)), ((),...]
  transfers between devices with their start and end apart: 3 -> 0, of which waited for: 2 -> 0; matrix products, arithmetic and copies ran while one was open for 2% -> 0% of each run, Pallas kernels for 52% -> 0%
where the time goes in v2:
time: 279 us; the launch traced here: 278 us
  Pallas kernels  268 us (96%)
  local copies, waits for them, and re-layouts  6.11 us (2%)
  between operations  3.89 us (1%)
    pallas_call x1, Pallas kernels, project(): pl.pallas_call(project_kernel, name='project', out_shape=(jax.ShapeDtypeS...  117 us
    pallas_call x1, Pallas kernels, attend(): pl.pallas_call(attend_kernel, name='attend', out_shape=(jax.ShapeDtypeStr...  105 us
    pallas_call x1, Pallas kernels, student(): pl.pallas_call(student_kernel, name='student', out_shape=(jax.ShapeDtypeS...  45 us

profile of v2, /device:TPU:1, one launch (start us, length us, event | category | flops | bytes accessed | tf_op | source)
XLA Modules:
  0.0 278.4 jit_solution(7089023271901626889)
XLA Ops:
  0.7 1.3 fusion
  2.0 0.0 copy-start
  2.0 0.0 copy-start.2
  2.0 0.0 copy-start.3
  2.0 0.0 copy-start.4
  2.0 117.5 %project.1 = (bf16[6,1024,256]{2,1,0:T(8,128)(2,1)}, bf16[4,256,3584]{2,1,0:T(8,128)(2,1)}) custom-call(bf16[128,7168]{1,0:T(8,128)(2,1)} %hid_hbm.1, f32[1,7168]{1,0:T(1,128)} %bitcast.12, bf16[3,7168,256]{2,1,0:T(8,128)(2,1)} %w_hbm.1, bf16[256,3584]{1,0:T(8,128)(2,1)} %wout_hbm.1), custom_call_target="tpu_custom_call" | custom-call | tf_op jit(solution)/shard_map/project/pallas_call | solution.py:273
  119.5 0.0 copy-done
  119.5 0.0 copy-done.2
  119.5 0.0 copy-done.3
  119.5 0.0 copy-done.4
  119.5 0.0 copy-start.5
  119.5 105.2 %attend.1 = (bf16[128,3584]{1,0:T(8,128)(2,1)S(1)}, bf16[4,8,2,224,256]{4,3,2,1,0:T(8,128)(2,1)}, bf16[2,8,128,1024]{3,2,1,0:T(8,128)(2,1)}) custom-call(s32[1]{0:T(128)} %get-tuple-element.20.len_ref, bf16[6,1024,256]{2,1,0:T(8,128)(2,1)} %get-tuple-element.12.qkv_ref, bf16[4,256,3584]{2,1,0:T(8,128)(2,1)} %get-tuple-element.13.wout_ref, ...), custom_call_target="tpu_custom_call" | custom-call | tf_op jit(solution)/shard_map/attend/pallas_call | solution.py:512
  224.8 0.0 copy-done.5
  224.8 0.6 reduce_sum.9
  226.8 0.0 copy-start.1
  226.8 2.2 copy-done.1
  228.9 45.0 %student.1 = (bf16[128,1024]{1,0:T(8,128)(2,1)S(1)}, bf16[224,1024]{1,0:T(8,128)(2,1)S(1)}, f32[16,128]{1,0:T(8,128)S(1)}) custom-call(s32[1]{0:T(128)} %get-tuple-element.21.len_ref, f32[1]{0:T(128)S(6)} %div.21.factor_ref, bf16[128,3584]{1,0:T(8,128)(2,1)S(1)} %get-tuple-element.14.target_ref, bf16[128,1024]{1,0:T(8,128)(2,1)S(1)} %copy-done.2, ...), custom_call_target="tpu_custom_call" | custom-call | tf_op jit(solution)/shard_map/student/pallas_call | solution.py:723
  274.0 0.6 slice_bitcast_fusion
  274.6 0.5 slice.7
  275.8 0.7 copy.16
  276.5 0.8 copy.17
Async XLA Ops:
  2.0 117.5 %copy-start = (bf16[128,7168]{1,0:T(8,128)(2,1)S(1)}, bf16[128,7168]{1,0:T(8,128)(2,1)}, u32[]{:S(2)}) copy-start(bf16[128,7168]{1,0:T(8,128)(2,1)} %hid_hbm.1) | copy-start | bytes 5505028
  2.0 117.5 %copy-start.2 = (bf16[128,1024]{1,0:T(8,128)(2,1)S(1)}, bf16[128,1024]{1,0:T(8,128)(2,1)}, u32[]{:S(2)}) copy-start(bf16[128,1024]{1,0:T(8,128)(2,1)} %student_ref.3) | copy-start | bytes 786436
  2.0 117.5 %copy-start.3 = (bf16[224,1024]{1,0:T(8,128)(2,1)S(1)}, bf16[224,1024]{1,0:T(8,128)(2,1)}, u32[]{:S(2)}) copy-start(bf16[224,1024]{1,0:T(8,128)(2,1)} %proj_ref.1) | copy-start | bytes 1376260
  2.0 117.5 %copy-start.4 = (f32[1024]{0:T(1024)S(1)}, f32[1024]{0:T(1024)}, u32[]{:S(2)}) copy-start(f32[1024]{0:T(1024)} %param.15) | copy-start | bytes 12292
  119.5 105.3 %copy-start.5 = (s32[16]{0:T(128)S(1)}, s32[16]{0:T(128)}, u32[]{:S(2)}) copy-start(s32[16]{0:T(128)} %param.13) | copy-start | bytes 196
  226.8 2.2 copy-start.1

commit v3 on v2

v3 whole, which is shorter than its diff:
```python
import functools
import math

import jax
import jax.numpy as jnp
from jax import lax
from jax.experimental import pallas as pl
from jax.experimental.pallas import tpu as pltpu
from jax.sharding import PartitionSpec as P

HEAD = 128
HW = 3584
LEN = 1024
SEQS = 2
D = 7168
DS = 1024
PROJ = 224
ROWS = 128
FIRST = 80
MESH = pl.DeviceIdType.MESH
MIB = 1 << 20


def place():
    tp = lax.axis_index("tp")
    return tp // 4, (tp // 2) % 2, tp % 2


def at(z, x, core):
    return {"tp": (z % 4) * 4 + x * 2 + core}


def across(z, x, core):
    dp = lax.axis_index("dp")
    return {"tp": z * 4 + (1 - x) * 2 + core, "dp": (1 - dp // 4) * 4 + dp % 4}


def beside(z, x, core, i):
    dp = lax.axis_index("dp")
    return {"tp": z * 4 + x * 2 + core, "dp": dp // 4 * 4 + (dp + i) % 4}


def remote(src, dst, send, recv, device):
    return pltpu.make_async_remote_copy(
        src_ref=src, dst_ref=dst, send_sem=send, recv_sem=recv, device_id=device, device_id_type=MESH
    )


def rms_norm(rows, gain):
    return rows * lax.rsqrt(jnp.mean(rows * rows, axis=-1, keepdims=True) + 1e-06) * gain


def greet(devices):
    barrier = pltpu.get_barrier_semaphore()
    for device in devices:
        pl.semaphore_signal(barrier, 1, device_id=device, device_id_type=MESH)
    pl.semaphore_wait(barrier, len(devices))


def project_kernel(
    x_ref,
    gain_ref,
    w_hbm,
    wout_hbm,
    proj_hbm,
    qkv_ref,
    wout_all,
    proj_all,
    normed,
    rows,
    w,
    send,
    recv,
    wsend,
    wrecv,
    psend,
    precv,
    ysend,
    yrecv,
    local,
):
    z, x, core = place()
    other = 1 - x
    kept = z // 2
    rel = (z - 2 * core + 4) % 4
    ahead = (rel == 0) | (rel == 3)
    step = jnp.where(ahead, 1, -1)
    near = (z + step + 4) % 4
    onward = (z - step + 4) % 4
    via = jnp.where(ahead, 1, 0)
    far = (z + 2) % 4

    greet(
        [at(z, x, 1 - core)]
        + [at(zz, x, c) for zz in (z + 1, z + 3) for c in (0, 1)]
        + [at(z, other, c) for c in (0, 1)]
        + [across(z, x, c) for c in (0, 1)]
        + [at(far, x, core)]
        + [beside(z, x, core, i) for i in (1, 2, 3)]
    )

    y = lax.axis_index("dp") % 4

    def held(chip_z, chip_x):
        return proj_all.at[y, (chip_z % 4) * 2 + chip_x, core]

    def held_sem(chip_z, chip_x):
        return precv.at[(chip_z % 4) * 2 + chip_x]

    quarter = proj_hbm.at[:, pl.ds(pl.multiple_of(y * 256, 256), 256)]
    quarter_here = pltpu.make_async_copy(quarter, held(z, x), local.at[6])
    quarter_going = [
        remote(quarter, held(z, x), psend.at[i], held_sem(z, x), at(zz, xx, core))
        for i, (zz, xx) in enumerate(((z + 1, x), (z + 3, x), (z + 2, x), (z, other)))
    ]
    for copy in [quarter_here] + quarter_going:
        copy.start()

    def quarter_wait(chip_z, chip_x):
        ref = held(chip_z, chip_x)
        remote(ref, ref, psend.at[0], held_sem(chip_z, chip_x), at(z, other, core)).wait_recv()

    def quarter_on(i):
        ref = held(z + i, x)
        return remote(ref, ref, psend.at[3 + i], held_sem(z + i, x), at(z, other, core))

    def along(i):
        ref = proj_all.at[y, :, core]
        return remote(ref, ref, ysend.at[i - 1], yrecv.at[y], beside(z, x, core, i))

    def halves(c):
        ref = proj_all.at[:, :, c]
        return remote(ref, ref, ysend.at[3], yrecv.at[4], at(z, x, 1 - core))

    w_out_going = [
        remote(w_hbm.at[k], w.at[core, k], wsend.at[k], wrecv.at[k], at(z, x, 1 - core)) for k in range(3)
    ]
    w_own = [pltpu.make_async_copy(w_hbm.at[k], w.at[core, k], local.at[k]) for k in range(3)]
    slot = x * 2 + core
    proj_going = [
        remote(wout_hbm, wout_all.at[slot], wsend.at[3], wrecv.at[3 + core], at(z, x, 1 - core)),
        remote(wout_hbm, wout_all.at[slot], wsend.at[4], wrecv.at[5 + core], across(z, x, 0)),
        remote(wout_hbm, wout_all.at[slot], wsend.at[5], wrecv.at[5 + core], across(z, x, 1)),
    ]
    proj_own = pltpu.make_async_copy(wout_hbm, wout_all.at[slot], local.at[3])
    for copy in w_own + w_out_going + proj_going + [proj_own]:
        copy.start()

    def part(chunk_z, chunk_x, s, cls):
        chunk = (chunk_z % 2) * 2 + chunk_x
        start, size = ((0, FIRST), (FIRST, ROWS - FIRST))[cls]
        return rows.at[chunk, pl.ds(pl.multiple_of(s * ROWS + start, 16), size)]

    def sem(chunk_z, chunk_x, s, cls):
        return recv.at[((chunk_z % 2) * 2 + chunk_x) * 4 + s * 2 + cls]

    def arrived(chunk_z, chunk_x, s, cls):
        ref = part(chunk_z, chunk_x, s, cls)
        remote(ref, ref, send.at[0], sem(chunk_z, chunk_x, s, cls), at(z, x, 1 - core)).wait_recv()

    def forward(chunk_z, chunk_x, s, cls, index, device):
        ref = part(chunk_z, chunk_x, s, cls)
        return remote(ref, ref, send.at[index], sem(chunk_z, chunk_x, s, cls), device)

    def norm(start, size):
        def one(i, carry):
            block = pl.ds(pl.multiple_of(start + i * 16, 16), 16)
            values = x_ref[block, :].astype(jnp.float32)
            centred = values - jnp.mean(values, axis=-1, keepdims=True)
            spread = jnp.mean(centred * centred, axis=-1, keepdims=True)
            normed[block, :] = (centred * lax.rsqrt(spread + 1e-05) * gain_ref[...]).astype(jnp.bfloat16)
            return carry

        lax.fori_loop(0, size // 16, one, 0)

    def own_copies(cls):
        start, size = ((0, FIRST), (FIRST, ROWS - FIRST))[cls]
        src = normed.at[pl.ds(start, size)]
        dst = part(z, x, core, cls)
        got = sem(z, x, core, cls)
        base = cls * 4
        return (
            [
                remote(src, dst, send.at[base], got, at(z + 1, x, kept)),
                remote(src, dst, send.at[base + 1], got, at(z + 3, x, kept)),
                remote(src, dst, send.at[base + 2], got, at(z, other, kept)),
            ],
            remote(src, dst, send.at[base + 3], got, at(z, x, 1 - core)),
            pltpu.make_async_copy(src, dst, local.at[4 + cls]),
        )

    for cls, (start, size) in ((1, (FIRST, ROWS - FIRST)), (0, (0, FIRST))):
        norm(start, size)
        away, sibling, here = own_copies(cls)
        for copy in away:
            copy.start()

        @pl.when(core == kept)
        def _():
            here.start()

        @pl.when(core != kept)
        def _():
            sibling.start()

    def multiply(chunk_z, chunk_x):
        chunk = (chunk_z % 2) * 2 + chunk_x

        def one(n, carry):
            out = jnp.dot(rows[chunk], w[n % 2, n // 2], preferred_element_type=jnp.float32)
            qkv_ref[n, pl.ds(pl.multiple_of(chunk * 256, 256), 256), :] = out.astype(jnp.bfloat16)
            return carry

        lax.fori_loop(0, 6, one, 0)

    for i in (1, 3, 2):
        quarter_wait(z + i, x)
        quarter_on(i).start()

    source = rel < 2

    fx = []
    for s in (0, 1):
        arrived(near, x, s, 1)
        fx.append(forward(near, x, s, 1, 8 + s, at(z, other, core)))
        fx[-1].start()
    on_b = forward(near, x, via, 1, 10, at(onward, x, core))
    on_b.start()

    for copy in w_own:
        copy.wait()
    for k in range(3):
        remote(w_hbm.at[k], w.at[1 - core, k], wsend.at[k], wrecv.at[k], at(z, x, 1 - core)).wait_recv()

    @pl.when(source)
    def _():
        for cls in (0, 1):
            arrived(z, x, 1 - core, cls)
            own_copies(cls)[2].wait()
        multiply(z, x)

    quarter_here.wait()
    for i in range(4):
        quarter_wait(z + i, other)
    for i in (1, 2, 3):
        along(i).start()

    for s in (0, 1):
        arrived(near, x, s, 0)
    on_a = forward(near, x, via, 0, 11, at(onward, x, core))
    on_a.start()

    def spread():
        return [
            forward(z, other, s, 0, 12 + s * 2 + i, at(zz, x, core))
            for s in (0, 1)
            for i, zz in enumerate((z + 1, z + 3))
        ]

    def crossing():
        return [forward(far, x, s, 1, 12 + s, at(z, other, core)) for s in (0, 1)]

    @pl.when(source)
    def _():
        for s in (0, 1):
            arrived(z, other, s, 0)
        for copy in spread():
            copy.start()
        for s in (0, 1):
            arrived(z, other, s, 1)
        multiply(z, other)

    @pl.when(jnp.logical_not(source))
    def _():
        for s in (0, 1):
            arrived(far, x, s, 1)
        for copy in crossing():
            copy.start()
        multiply(near, x)

    for s in (0, 1):
        arrived(near, other, s, 0)
    on_p = forward(near, other, via, 0, 16, at(onward, x, core))
    on_p.start()

    @pl.when(source)
    def _():
        multiply(near, x)

    for s in (0, 1):
        arrived(near, other, s, 1)
    multiply(near, other)

    for i in (1, 2, 3):
        ref = proj_all.at[(y + i) % 4, :, core]
        remote(ref, ref, ysend.at[0], yrecv.at[(y + i) % 4], at(z, x, 1 - core)).wait_recv()
    halves(core).start()

    @pl.when(jnp.logical_not(source))
    def _():
        for s in (0, 1):
            arrived(far, x, s, 0)
        multiply(far, x)
        for s in (0, 1):
            arrived(far, other, s, 0)
            arrived(far, other, s, 1)
        multiply(far, other)

    for cls in (0, 1):
        away, sibling, here = own_copies(cls)
        for copy in away:
            copy.wait_send()

        @pl.when(core != kept)
        def _():
            sibling.wait_send()

    for copy in fx + [on_b, on_a, on_p]:
        copy.wait_send()

    @pl.when(source)
    def _():
        for copy in spread():
            copy.wait_send()

    @pl.when(jnp.logical_not(source))
    def _():
        for copy in crossing():
            copy.wait_send()

    for copy in w_out_going + proj_going + quarter_going + [quarter_on(i) for i in (1, 2, 3)]:
        copy.wait_send()
    for copy in [along(i) for i in (1, 2, 3)] + [halves(core)]:
        copy.wait_send()
    halves(1 - core).wait_recv()
    proj_own.wait()
    remote(
        wout_hbm, wout_all.at[x * 2 + 1 - core], wsend.at[3], wrecv.at[3 + 1 - core], at(z, x, 1 - core)
    ).wait_recv()
    for c in (0, 1):
        remote(wout_hbm, wout_all.at[other * 2 + c], wsend.at[4], wrecv.at[5 + c], across(z, x, c)).wait_recv()


def project(hidden, gain, w_qkv, w_out, proj):
    vmem = pl.BlockSpec(memory_space=pltpu.VMEM)
    hbm = pl.BlockSpec(memory_space=pltpu.HBM)
    return pl.pallas_call(
        project_kernel,
        name="project",
        out_shape=(
            jax.ShapeDtypeStruct((6, LEN, 256), jnp.bfloat16),
            jax.ShapeDtypeStruct((4, 256, HW), jnp.bfloat16),
            jax.ShapeDtypeStruct((4, 8, 2, PROJ, 256), jnp.bfloat16),
        ),
        in_specs=[vmem, vmem, hbm, hbm, hbm],
        out_specs=(vmem, hbm, hbm),
        scratch_shapes=[
            pltpu.VMEM((ROWS, D), jnp.bfloat16),
            pltpu.VMEM((4, 2 * ROWS, D), jnp.bfloat16),
            pltpu.VMEM((2, 3, D, 256), jnp.bfloat16),
        ]
        + [pltpu.SemaphoreType.DMA((n,)) for n in (17, 16, 6, 7, 7, 8, 4, 5, 7)],
        compiler_params=pltpu.CompilerParams(
            collective_id=0, has_side_effects=True, vmem_limit_bytes=60 * MIB
        ),
    )(hidden, gain, w_qkv, w_out, proj)


def student_kernel(
    key_len_ref,
    row_len_ref,
    factor_ref,
    qkv_ref,
    wout_hbm,
    hid_hbm,
    proj_hbm,
    student_ref,
    gain_ref,
    grad_ref,
    out_ref,
    stat_ref,
    wout_ref,
    hid_ref,
    proj_ref,
    norm_ref,
    normed,
    ctx,
    ctx_in,
    stage,
    parts,
    mapped,
    delta,
    flipped,
    flipped_in,
    stat,
    stat_in,
    total,
    total_in,
    piece,
    piece_in,
    summed,
    send,
    recv,
    osend,
    orecv,
    nsend,
    nrecv,
    dsend,
    drecv,
    ssend,
    srecv,
    tsend,
    trecv,
    gsend,
    grecv,
    asend,
    arecv,
    local,
):
    z, x, core = place()
    other = 1 - x
    kept = z // 2
    tp = lax.axis_index("tp")
    dp = lax.axis_index("dp")
    factor = factor_ref[0]
    key_len = key_len_ref[0]

    fetch_wout = pltpu.make_async_copy(wout_hbm, wout_ref, local.at[0])
    fetch_hid = pltpu.make_async_copy(hid_hbm.at[:, pl.ds(0, HW)], hid_ref, local.at[1])
    fetch_proj = pltpu.make_async_copy(proj_hbm, proj_ref, local.at[2])
    for copy in (fetch_wout, fetch_hid, fetch_proj):
        copy.start()

    def mate(i):
        return (tp + i) % 16

    def group(i):
        return (dp + i) % 8

    greet([{"tp": mate(i)} for i in range(1, 16)] + [{"dp": group(i)} for i in range(1, 8)])

    rows = student_ref[...].astype(jnp.float32)
    scale = lax.rsqrt(jnp.mean(rows * rows, axis=-1, keepdims=True) + 1e-06)
    normed[...] = (rows * scale * gain_ref[...]).astype(jnp.bfloat16)

    def block(chip_z, chip_x, c):
        chip = (chip_z % 4) * 2 + chip_x
        return norm_ref.at[pl.ds(pl.multiple_of((c * 8 + chip) * ROWS, 128), ROWS)]

    def block_sem(chip_z, chip_x):
        return nrecv.at[(chip_z % 4) * 2 + chip_x]

    norm_here = pltpu.make_async_copy(normed, block(z, x, core), local.at[3])
    norm_going = [
        remote(normed, block(z, x, core), nsend.at[i], block_sem(z, x), at(zz, xx, core))
        for i, (zz, xx) in enumerate(((z + 1, x), (z + 3, x), (z + 2, x), (z, other)))
    ]
    for copy in [norm_here] + norm_going:
        copy.start()

    def norm_wait(chip_z, chip_x):
        ref = block(chip_z, chip_x, core)
        remote(ref, ref, nsend.at[0], block_sem(chip_z, chip_x), at(z, other, core)).wait_recv()

    def norm_on(i):
        ref = block(z + i, x, core)
        return remote(ref, ref, nsend.at[3 + i], block_sem(z + i, x), at(z, other, core))

    def norm_half(c):
        ref = norm_ref.at[pl.ds(pl.multiple_of(c * LEN, 128), LEN)]
        return remote(ref, ref, nsend.at[7], nrecv.at[8], at(z, x, 1 - core))

    def attend(chunk, keys, zq, mine):
        start = pl.multiple_of(chunk * 256, 256)
        row = lax.broadcasted_iota(jnp.int32, (256, keys), 0) + start
        col = lax.broadcasted_iota(jnp.int32, (256, keys), 1)
        allowed = (col <= row) & (col < key_len)

        def pair(half, carry):
            for h in (0, 1):
                lanes = slice(h * HEAD, (h + 1) * HEAD)
                q = qkv_ref[half, pl.ds(start, 256), lanes]
                k = qkv_ref[2 + half, :keys, lanes]
                v = qkv_ref[4 + half, :keys, lanes]
                scores = lax.dot_general(
                    q, k, (((1,), (1,)), ((), ())), preferred_element_type=jnp.float32
                ) * (1.0 / math.sqrt(HEAD))
                scores = jnp.where(allowed, scores, -1e30)
                weights = jnp.exp(scores - jnp.max(scores, axis=-1, keepdims=True))
                norm = jnp.sum(weights, axis=-1, keepdims=True)
                out = jnp.dot(weights.astype(jnp.bfloat16), v, preferred_element_type=jnp.float32)
                ctx[zq * 2 + mine, half, :, lanes] = (out / norm).astype(jnp.bfloat16)
            return carry

        lax.fori_loop(0, 2, pair, 0)

    def swap(zq):
        return remote(ctx.at[zq * 2], ctx_in.at[zq], send.at[zq], recv.at[zq], at(z, other, core))

    def give(zq, s):
        return remote(
            stage.at[zq, pl.ds(s * ROWS, ROWS)],
            parts.at[z],
            osend.at[zq * 2 + s],
            orecv.at[z],
            at(2 * core + zq, x, s),
        )

    def keep(zq, s):
        return pltpu.make_async_copy(stage.at[zq, pl.ds(s * ROWS, ROWS)], parts.at[z], osend.at[zq * 2 + s])

    def project_out(zq):
        def one(n, carry):
            lanes = pl.ds(pl.multiple_of(n * 512, 512), 512)
            out = jnp.zeros((256, 512), jnp.float32)
            for half in (0, 1):
                out += jnp.dot(
                    ctx[zq * 2 + 1, half], wout_ref[x * 2 + half, :, lanes], preferred_element_type=jnp.float32
                )
                out += jnp.dot(
                    ctx_in[zq, half], wout_ref[other * 2 + half, :, lanes], preferred_element_type=jnp.float32
                )
            stage[zq, :, lanes] = out.astype(jnp.bfloat16)
            return carry

        lax.fori_loop(0, HW // 512, one, 0)
        for s in (0, 1):
            mine = (2 * core + zq == z) & (core == s)

            @pl.when(mine)
            def _():
                keep(zq, s).start()

            @pl.when(jnp.logical_not(mine))
            def _():
                give(zq, s).start()

    attend(other, 512, 0, 0)
    swap(0).start()
    attend(x, 512, 0, 1)
    for i in (1, 3, 2):
        norm_wait(z + i, x)
        norm_on(i).start()
    fetch_wout.wait()
    swap(0).wait_recv()
    project_out(0)
    attend(2 + other, 1024, 1, 0)
    swap(1).start()
    attend(2 + x, 1024, 1, 1)
    swap(1).wait_recv()
    project_out(1)
    norm_here.wait()
    for i in range(4):
        norm_wait(z + i, other)
    norm_half(core).start()

    fetch_proj.wait()

    def map_rows(n, carry):
        base = pl.multiple_of(n * 512, 512)
        out = jnp.zeros((ROWS, 512), jnp.float32)
        for k in range(4):
            out += lax.dot_general(
                normed[:, k * 256 : (k + 1) * 256],
                proj_ref[k, pl.ds(base, 512), :],
                (((1,), (1,)), ((), ())),
                preferred_element_type=jnp.float32,
            )
        mapped[:, pl.ds(base, 512)] = out
        return carry

    lax.fori_loop(0, HW // 512, map_rows, 0)
    fetch_hid.wait()

    for far in (0, 1, 2, 3):

        @pl.when((z != far) | (core != kept))
        def _():
            remote(
                parts.at[far], parts.at[far], osend.at[0], orecv.at[far], at(z, x, 1 - core)
            ).wait_recv()

    for zq in (0, 1):
        mine = (2 * core + zq == z) & (core == kept)

        @pl.when(mine)
        def _():
            pltpu.make_async_copy(
                stage.at[zq, pl.ds(pl.multiple_of(core * ROWS, 16), ROWS)], parts.at[z], osend.at[zq * 2 + core]
            ).wait()

    position = (tp % 8) * ROWS + lax.broadcasted_iota(jnp.int32, (ROWS, 1), 0)
    valid = position < row_len_ref[0]

    def compare(n, loss):
        cols = pl.ds(pl.multiple_of(n * 512, 512), 512)
        mixed = parts[0, :, cols].astype(jnp.float32)
        for far in (1, 2, 3):
            mixed += parts[far, :, cols].astype(jnp.float32)
        target = (hid_ref[:, cols].astype(jnp.float32) + mixed).astype(jnp.bfloat16)
        diff = jnp.where(valid, mapped[:, cols] - target.astype(jnp.float32), 0.0)
        scaled = diff * factor
        delta[:, cols] = scaled.astype(jnp.bfloat16)
        for t in range(4):
            tile = scaled[:, t * 128 : (t + 1) * 128]
            flipped[pl.ds(pl.multiple_of(n * 512 + t * 128, 128), 128), :] = tile.T.astype(jnp.bfloat16)
        return loss + jnp.sum(diff * diff)

    loss = lax.fori_loop(0, HW // 512, compare, jnp.float32(0.0))

    lane = pl.ds(pl.multiple_of((core * 8 + z * 2 + x) * ROWS, 128), ROWS)

    def flip(i):
        src = flipped.at[pl.ds(pl.multiple_of(mate(i) * PROJ, 16), PROJ)]
        return remote(src, flipped_in.at[:, lane], dsend.at[i - 1], drecv.at[tp], {"tp": mate(i)})

    own_flip = pltpu.make_async_copy(
        flipped.at[pl.ds(pl.multiple_of(tp * PROJ, 16), PROJ)], flipped_in.at[:, lane], local.at[4]
    )
    for i in range(1, 16):
        flip(i).start()
    own_flip.start()

    back = [jnp.dot(delta[...], proj_ref[k], preferred_element_type=jnp.float32) for k in range(4)]
    dots = jnp.zeros((ROWS, 1), jnp.float32)
    for k in range(4):
        cols = slice(k * 256, (k + 1) * 256)
        dots += jnp.sum(back[k] * gain_ref[:, cols] * rows[:, cols], axis=-1, keepdims=True)
    shift = dots * (scale * scale * scale) * (1.0 / DS)
    for k in range(4):
        cols = slice(k * 256, (k + 1) * 256)
        grad_ref[:, cols] = (
            back[k] * gain_ref[:, cols] * scale - rows[:, cols] * shift
        ).astype(jnp.bfloat16)
        part = jnp.sum(back[k] * (rows[:, cols] * scale), axis=0, keepdims=True)
        stat[2 * k : 2 * k + 1, :] = part[:, :128]
        stat[2 * k + 1 : 2 * k + 2, :] = part[:, 128:]
    stat[8:16, :] = jnp.zeros((8, 128), jnp.float32) + loss

    def tell(i):
        return remote(stat, stat_in.at[tp], ssend.at[i - 1], srecv.at[tp], {"tp": mate(i)})

    for i in range(1, 16):
        tell(i).start()

    norm_half(1 - core).wait_recv()
    for i in range(1, 16):
        far = mate(i)
        got = flipped_in.at[:, pl.ds(pl.multiple_of(((far % 2) * 8 + far // 2) * ROWS, 128), ROWS)]
        remote(got, got, dsend.at[0], drecv.at[far], {"tp": far}).wait_recv()
    own_flip.wait()

    def hand(i):
        return remote(piece.at[group(i)], piece_in.at[dp], gsend.at[i - 1], grecv.at[dp], {"dp": group(i)})

    for k in range(4):
        out = jnp.dot(
            flipped_in[...], norm_ref[:, k * 256 : (k + 1) * 256], preferred_element_type=jnp.float32
        ).astype(jnp.bfloat16)
        piece[2 * k] = out[:, :128]
        piece[2 * k + 1] = out[:, 128:]
    for i in range(1, 8):
        hand(i).start()

    for i in range(1, 16):
        far = stat_in.at[mate(i)]
        remote(far, far, ssend.at[0], srecv.at[mate(i)], {"tp": mate(i)}).wait_recv()
    stat_in[tp] = stat[...]
    total[...] = jnp.sum(stat_in[...], axis=0)

    def tell_groups(i):
        return remote(total, total_in.at[dp], tsend.at[i - 1], trecv.at[dp], {"dp": group(i)})

    for i in range(1, 8):
        tell_groups(i).start()

    for i in range(1, 8):
        far = piece_in.at[group(i)]
        remote(far, far, gsend.at[0], grecv.at[group(i)], {"dp": group(i)}).wait_recv()
    piece_in[dp] = piece[dp]
    acc = jnp.zeros((PROJ, 128), jnp.float32)
    for k in range(8):
        acc += piece_in[k].astype(jnp.float32)
    summed[...] = acc.astype(jnp.bfloat16)

    def column(g):
        return out_ref.at[:, pl.ds(pl.multiple_of(g * 128, 128), 128)]

    def publish(i):
        return remote(summed, column(dp), asend.at[i - 1], arecv.at[dp], {"dp": group(i)})

    own_column = pltpu.make_async_copy(summed, column(dp), local.at[5])
    own_column.start()
    for i in range(1, 8):
        publish(i).start()

    for i in range(1, 8):
        far = total_in.at[group(i)]
        remote(far, far, tsend.at[0], trecv.at[group(i)], {"dp": group(i)}).wait_recv()
    total_in[dp] = total[...]
    stat_ref[...] = jnp.sum(total_in[...], axis=0)

    for zq in (0, 1):
        swap(zq).wait_send()
        for s in (0, 1):

            @pl.when((2 * core + zq != z) | (core != s))
            def _():
                give(zq, s).wait_send()

    for copy in norm_going + [norm_on(i) for i in (1, 2, 3)] + [norm_half(core)]:
        copy.wait_send()
    for i in range(1, 16):
        flip(i).wait_send()
        tell(i).wait_send()
    for i in range(1, 8):
        hand(i).wait_send()
        tell_groups(i).wait_send()
    for i in range(1, 8):
        far = column(group(i))
        remote(far, far, asend.at[0], arecv.at[group(i)], {"dp": group(i)}).wait_recv()
        publish(i).wait_send()
    own_column.wait()


def student(key_len, row_len, factor, qkv, w_out, hidden, proj, rows, gain):
    vmem = pl.BlockSpec(memory_space=pltpu.VMEM)
    smem = pl.BlockSpec(memory_space=pltpu.SMEM)
    hbm = pl.BlockSpec(memory_space=pltpu.HBM)
    return pl.pallas_call(
        student_kernel,
        name="student",
        out_shape=(
            jax.ShapeDtypeStruct((ROWS, DS), jnp.bfloat16),
            jax.ShapeDtypeStruct((PROJ, DS), jnp.bfloat16),
            jax.ShapeDtypeStruct((16, 128), jnp.float32),
        ),
        in_specs=[smem, smem, smem, vmem, hbm, hbm, hbm, vmem, vmem],
        out_specs=(vmem, vmem, vmem),
        scratch_shapes=[
            pltpu.VMEM((4, 256, HW), jnp.bfloat16),
            pltpu.VMEM((ROWS, HW), jnp.bfloat16),
            pltpu.VMEM((4, HW, 256), jnp.bfloat16),
            pltpu.VMEM((2 * LEN, DS), jnp.bfloat16),
            pltpu.VMEM((ROWS, DS), jnp.bfloat16),
            pltpu.VMEM((4, 2, 256, 256), jnp.bfloat16),
            pltpu.VMEM((2, 2, 256, 256), jnp.bfloat16),
            pltpu.VMEM((2, 256, HW), jnp.bfloat16),
            pltpu.VMEM((4, ROWS, HW), jnp.bfloat16),
            pltpu.VMEM((ROWS, HW), jnp.float32),
            pltpu.VMEM((ROWS, HW), jnp.bfloat16),
            pltpu.VMEM((HW, ROWS), jnp.bfloat16),
            pltpu.VMEM((PROJ, 2 * LEN), jnp.bfloat16),
            pltpu.VMEM((16, 128), jnp.float32),
            pltpu.VMEM((16, 16, 128), jnp.float32),
            pltpu.VMEM((16, 128), jnp.float32),
            pltpu.VMEM((8, 16, 128), jnp.float32),
            pltpu.VMEM((8, PROJ, 128), jnp.bfloat16),
            pltpu.VMEM((8, PROJ, 128), jnp.bfloat16),
            pltpu.VMEM((PROJ, 128), jnp.bfloat16),
        ]
        + [pltpu.SemaphoreType.DMA((n,)) for n in (2, 2, 4, 4, 8, 9, 15, 16, 15, 16, 7, 8, 7, 8, 7, 8, 6)],
        compiler_params=pltpu.CompilerParams(
            collective_id=1, has_side_effects=True, vmem_limit_bytes=56 * MIB
        ),
    )(key_len, row_len, factor, qkv, w_out, hidden, proj, rows, gain)


def shards(
    hidden_in, norm_gain, w_qkv, w_out, lengths, student_in, student_gain, proj_weight, loss_scale
):
    tp = lax.axis_index("tp")
    group = lax.axis_index("dp")
    count = jnp.sum(lengths).astype(jnp.float32)
    factor = 2.0 * loss_scale / (count * HW)
    gain = student_gain.reshape(1, DS)

    qkv, w_out_all, proj_all = project(hidden_in, norm_gain.reshape(1, D), w_qkv, w_out, proj_weight)
    row_grad, proj_grad, stat = student(
        lax.dynamic_slice_in_dim(lengths, group * SEQS + tp % 2, 1),
        lax.dynamic_slice_in_dim(lengths, group * SEQS + tp // 8, 1),
        factor,
        qkv,
        w_out_all,
        hidden_in,
        proj_all.reshape(4, HW, 256),
        student_in,
        gain,
    )
    return row_grad, proj_grad, stat[:8].reshape(DS), stat[8, 0] / (count * HW)


def solution(mesh):
    placed = (
        P(("dp", "tp"), None),
        P(),
        P(None, None, "tp"),
        P("tp", None),
        P(),
        P(("dp", "tp"), None),
        P(),
        P("tp", None),
        P(),
    )
    return jax.shard_map(
        shards,
        mesh=mesh,
        in_specs=placed,
        out_specs=(P(("dp", "tp"), None), P("tp", None), P(), P()),
        check_vma=False,
    )
```

time: 279 us -> 257 us (0.921)
  Pallas kernels: 268 us -> 245 us
    pallas_call x1 -> x0, Pallas kernels: 105 us -> none  [attend(): pl.pallas_call(attend_kernel, name='attend', out_shape=(jax.ShapeDtypeStr...]
    pallas_call x1, Pallas kernels: 45 us -> 123 us  [student(): pl.pallas_call(student_kernel, name='student', out_shape=(jax.ShapeDtypeS...]
    pallas_call x1, Pallas kernels: 117 us -> 122 us  [project(): pl.pallas_call(project_kernel, name='project', out_shape=(jax.ShapeDtypeS...]
where the time goes in v3:
time: 257 us
  Pallas kernels  245 us (95%)
  local copies, waits for them, and re-layouts  7.27 us (3%)
  between operations  3.81 us (1%)
    pallas_call x1, Pallas kernels, student(): pl.pallas_call(student_kernel, name='student', out_shape=(jax.ShapeDtypeS...  123 us
    pallas_call x1, Pallas kernels, project(): pl.pallas_call(project_kernel, name='project', out_shape=(jax.ShapeDtypeS...  122 us

profile of v3, /device:TPU:1, one launch (start us, length us, event | category | flops | bytes accessed | tf_op | source)
XLA Modules:
  0.0 257.1 jit_solution(14492074330929421411)
XLA Ops:
  1.3 1.3 reduce_sum.9
  3.3 1.3 fusion
  4.6 121.7 %project.1 = (bf16[6,1024,256]{2,1,0:T(8,128)(2,1)}, bf16[4,256,3584]{2,1,0:T(8,128)(2,1)}, bf16[4,8,2,224,256]{4,3,2,1,0:T(8,128)(2,1)}) custom-call(bf16[128,7168]{1,0:T(8,128)(2,1)} %hid_hbm.1, f32[1,7168]{1,0:T(1,128)} %bitcast.8, bf16[3,7168,256]{2,1,0:T(8,128)(2,1)} %w_hbm.1, bf16[256,3584]{1,0:T(8,128)(2,1)} %wout_hbm.1, bf16[224,1024]{1,0:T(8,128)(2,1)} %proj_hbm.1), custom_call_target="tpu_custom_call" | custom-call | tf_op jit(solution)/shard_map/project/pallas_call | solution.py:347
  126.4 123.0 %student.1 = (bf16[128,1024]{1,0:T(8,128)(2,1)}, bf16[224,1024]{1,0:T(8,128)(2,1)}, f32[16,128]{1,0:T(8,128)}) custom-call(s32[1]{0:T(128)} %get-tuple-element.17.key_len_ref, s32[1]{0:T(128)} %get-tuple-element.16.row_len_ref, f32[1]{0:T(128)S(6)} %div.21.factor_ref, bf16[6,1024,256]{2,1,0:T(8,128)(2,1)} %get-tuple-element.10.qkv_ref, ...), custom_call_target="tpu_custom_call" | custom-call | tf_op jit(solution)/shard_map/student/pallas_call | solution.py:730
  249.3 1.2 slice.7
  251.2 1.3 slice_bitcast_fusion
  252.5 1.7 copy.16
  254.1 1.8 copy.17

commit v4 on v3

--- a/solution.py
+++ b/solution.py
@@ -10,6 +10,7 @@
 
 HEAD = 128
 HW = 3584
+HALF = HW // 2
 LEN = 1024
 SEQS = 2
 D = 7168
@@ -367,9 +368,8 @@
 
 
 def student_kernel(
-    key_len_ref,
-    row_len_ref,
-    factor_ref,
+    len_ref,
+    scale_ref,
     qkv_ref,
     wout_hbm,
     hid_hbm,
@@ -388,6 +388,7 @@
     ctx_in,
     stage,
     parts,
+    relay,
     mapped,
     delta,
     flipped,
@@ -403,6 +404,7 @@
     recv,
     osend,
     orecv,
+    rrecv,
     nsend,
     nrecv,
     dsend,
@@ -422,8 +424,17 @@
     kept = z // 2
     tp = lax.axis_index("tp")
     dp = lax.axis_index("dp")
-    factor = factor_ref[0]
-    key_len = key_len_ref[0]
+    rel = (z - 2 * core + 4) % 4
+    ahead = (rel == 0) | (rel == 3)
+    step = jnp.where(ahead, 1, -1)
+    via = jnp.where(ahead, 0, 1)
+    source = rel < 2
+    key_len = len_ref[dp * SEQS + core]
+    count = len_ref[0]
+    for i in range(1, len_ref.shape[0]):
+        count += len_ref[i]
+    terms = jnp.full((1, 128), 1.0, jnp.float32) * count.astype(jnp.float32) * HW
+    factor = (2.0 * scale_ref[0] / terms)[:, :1]
 
     fetch_wout = pltpu.make_async_copy(wout_hbm, wout_ref, local.at[0])
     fetch_hid = pltpu.make_async_copy(hid_hbm.at[:, pl.ds(0, HW)], hid_ref, local.at[1])
@@ -455,7 +466,7 @@
         remote(normed, block(z, x, core), nsend.at[i], block_sem(z, x), at(zz, xx, core))
         for i, (zz, xx) in enumerate(((z + 1, x), (z + 3, x), (z + 2, x), (z, other)))
     ]
-    for copy in [norm_here] + norm_going:
+    for copy in [norm_here] + norm_going[:3]:
         copy.start()
 
     def norm_wait(chip_z, chip_x):
@@ -497,62 +508,123 @@
     def swap(zq):
         return remote(ctx.at[zq * 2], ctx_in.at[zq], send.at[zq], recv.at[zq], at(z, other, core))
 
-    def give(zq, s):
+    def side(half):
+        return pl.ds(half * HALF, HALF)
+
+    def summand(zq, s, half):
+        return stage.at[zq, pl.ds(pl.multiple_of(s * ROWS, 16), ROWS), side(half)]
+
+    def give(zq, s, half):
+        slot = jnp.where(ahead, 2, 1)
         return remote(
-            stage.at[zq, pl.ds(s * ROWS, ROWS)],
-            parts.at[z],
-            osend.at[zq * 2 + s],
-            orecv.at[z],
-            at(2 * core + zq, x, s),
+            summand(zq, s, half),
+            parts.at[slot, :, side(half)],
+            osend.at[zq * 4 + s * 2 + half],
+            orecv.at[slot * 2 + half],
+            at(z + step + 4, x, s),
         )
 
-    def keep(zq, s):
-        return pltpu.make_async_copy(stage.at[zq, pl.ds(s * ROWS, ROWS)], parts.at[z], osend.at[zq * 2 + s])
-
-    def project_out(zq):
+    def pass_on(zq, s, half):
+        return remote(
+            summand(zq, s, half),
+            relay.at[:, side(half)],
+            osend.at[zq * 4 + s * 2 + half],
+            rrecv.at[half],
+            at(z + (1 if s == 0 else 3), x, core),
+        )
+
+    def hand_over(zq, half):
+        return remote(
+            summand(zq, 1 - core, half),
+            parts.at[0, :, side(half)],
+            osend.at[zq * 4 + (1 - core) * 2 + half],
+            orecv.at[half],
+            at(z, x, 1 - core),
+        )
+
+    def keep(zq, half):
+        return pltpu.make_async_copy(
+            summand(zq, core, half), parts.at[0, :, side(half)], osend.at[zq * 4 + core * 2 + half]
+        )
+
+    def is_near(zq):
+        return (rel == 1 - zq) | (rel == 3 - zq)
+
+    def is_far(zq):
+        return rel == 2 + zq
+
+    def is_own(zq):
+        return rel == zq
+
+    def project_out(zq, half):
         def one(n, carry):
-            lanes = pl.ds(pl.multiple_of(n * 512, 512), 512)
-            out = jnp.zeros((256, 512), jnp.float32)
-            for half in (0, 1):
+            lanes = pl.ds(pl.multiple_of(half * HALF + n * 896, 128), 896)
+            out = jnp.zeros((256, 896), jnp.float32)
+            for k in (0, 1):
                 out += jnp.dot(
-                    ctx[zq * 2 + 1, half], wout_ref[x * 2 + half, :, lanes], preferred_element_type=jnp.float32
+                    ctx[zq * 2 + 1, k], wout_ref[x * 2 + k, :, lanes], preferred_element_type=jnp.float32
                 )
                 out += jnp.dot(
-                    ctx_in[zq, half], wout_ref[other * 2 + half, :, lanes], preferred_element_type=jnp.float32
+                    ctx_in[zq, k], wout_ref[other * 2 + k, :, lanes], preferred_element_type=jnp.float32
                 )
             stage[zq, :, lanes] = out.astype(jnp.bfloat16)
             return carry
 
-        lax.fori_loop(0, HW // 512, one, 0)
-        for s in (0, 1):
-            mine = (2 * core + zq == z) & (core == s)
-
-            @pl.when(mine)
-            def _():
-                keep(zq, s).start()
-
-            @pl.when(jnp.logical_not(mine))
-            def _():
-                give(zq, s).start()
+        lax.fori_loop(0, HALF // 896, one, 0)
+
+        @pl.when(is_far(zq))
+        def _():
+            for s in (0, 1):
+                pass_on(zq, s, half).start()
+
+        @pl.when(is_near(zq))
+        def _():
+            give(zq, 1 - via, half).start()
+
+        @pl.when(is_own(zq))
+        def _():
+            keep(zq, half).start()
+            hand_over(zq, half).start()
+
+    def join(zq, half):
+        @pl.when(is_near(zq))
+        def _():
+            src = relay.at[:, side(half)]
+            remote(src, src, osend.at[0], rrecv.at[half], at(z, x, 1 - core)).wait_recv()
+
+            def one(i, carry):
+                here = pl.ds(pl.multiple_of(via * ROWS + i * 16, 16), 16)
+                there = pl.ds(pl.multiple_of(i * 16, 16), 16)
+                both = stage[zq, here, side(half)].astype(jnp.float32) + relay[there, side(half)].astype(
+                    jnp.float32
+                )
+                stage[zq, here, side(half)] = both.astype(jnp.bfloat16)
+                return carry
+
+            lax.fori_loop(0, ROWS // 16, one, 0)
+            give(zq, via, half).start()
 
     attend(other, 512, 0, 0)
     swap(0).start()
     attend(x, 512, 0, 1)
+    fetch_wout.wait()
+    swap(0).wait_recv()
+    for half in (0, 1):
+        project_out(0, half)
+    attend(2 + other, 1024, 1, 0)
+    swap(1).start()
+    attend(2 + x, 1024, 1, 1)
+    for half in (0, 1):
+        join(0, half)
+    swap(1).wait_recv()
+    for half in (0, 1):
+        project_out(1, half)
+    norm_going[3].start()
     for i in (1, 3, 2):
         norm_wait(z + i, x)
         norm_on(i).start()
-    fetch_wout.wait()
-    swap(0).wait_recv()
-    project_out(0)
-    attend(2 + other, 1024, 1, 0)
-    swap(1).start()
-    attend(2 + x, 1024, 1, 1)
-    swap(1).wait_recv()
-    project_out(1)
-    norm_here.wait()
-    for i in range(4):
-        norm_wait(z + i, other)
-    norm_half(core).start()
+    for half in (0, 1):
+        join(1, half)
 
     fetch_proj.wait()
 
@@ -572,54 +644,72 @@
     lax.fori_loop(0, HW // 512, map_rows, 0)
     fetch_hid.wait()
 
-    for far in (0, 1, 2, 3):
-
-        @pl.when((z != far) | (core != kept))
-        def _():
-            remote(
-                parts.at[far], parts.at[far], osend.at[0], orecv.at[far], at(z, x, 1 - core)
-            ).wait_recv()
-
-    for zq in (0, 1):
-        mine = (2 * core + zq == z) & (core == kept)
-
-        @pl.when(mine)
-        def _():
-            pltpu.make_async_copy(
-                stage.at[zq, pl.ds(pl.multiple_of(core * ROWS, 16), ROWS)], parts.at[z], osend.at[zq * 2 + core]
-            ).wait()
-
     position = (tp % 8) * ROWS + lax.broadcasted_iota(jnp.int32, (ROWS, 1), 0)
-    valid = position < row_len_ref[0]
-
-    def compare(n, loss):
-        cols = pl.ds(pl.multiple_of(n * 512, 512), 512)
-        mixed = parts[0, :, cols].astype(jnp.float32)
-        for far in (1, 2, 3):
-            mixed += parts[far, :, cols].astype(jnp.float32)
-        target = (hid_ref[:, cols].astype(jnp.float32) + mixed).astype(jnp.bfloat16)
-        diff = jnp.where(valid, mapped[:, cols] - target.astype(jnp.float32), 0.0)
-        scaled = diff * factor
-        delta[:, cols] = scaled.astype(jnp.bfloat16)
-        for t in range(4):
-            tile = scaled[:, t * 128 : (t + 1) * 128]
-            flipped[pl.ds(pl.multiple_of(n * 512 + t * 128, 128), 128), :] = tile.T.astype(jnp.bfloat16)
-        return loss + jnp.sum(diff * diff)
-
-    loss = lax.fori_loop(0, HW // 512, compare, jnp.float32(0.0))
-
+    valid = position < len_ref[dp * SEQS + kept]
     lane = pl.ds(pl.multiple_of((core * 8 + z * 2 + x) * ROWS, 128), ROWS)
 
-    def flip(i):
-        src = flipped.at[pl.ds(pl.multiple_of(mate(i) * PROJ, 16), PROJ)]
-        return remote(src, flipped_in.at[:, lane], dsend.at[i - 1], drecv.at[tp], {"tp": mate(i)})
+    def owner(half, i):
+        return half * 8 + (tp + i) % 8
+
+    def flip(half, i):
+        src = flipped.at[pl.ds(pl.multiple_of(owner(half, i) * PROJ, 16), PROJ)]
+        return remote(
+            src, flipped_in.at[:, lane], dsend.at[half * 8 + i], drecv.at[tp], {"tp": owner(half, i)}
+        )
 
     own_flip = pltpu.make_async_copy(
         flipped.at[pl.ds(pl.multiple_of(tp * PROJ, 16), PROJ)], flipped_in.at[:, lane], local.at[4]
     )
-    for i in range(1, 16):
-        flip(i).start()
-    own_flip.start()
+
+    def compare(n, loss):
+        block_cols = pl.ds(pl.multiple_of(n * 256, 256), 256)
+        mixed = parts[0, :, block_cols].astype(jnp.float32)
+        for slot in (1, 2):
+            mixed += parts[slot, :, block_cols].astype(jnp.float32)
+        target = (hid_ref[:, block_cols].astype(jnp.float32) + mixed).astype(jnp.bfloat16)
+        diff = jnp.where(valid, mapped[:, block_cols] - target.astype(jnp.float32), 0.0)
+        scaled = diff * factor
+        delta[:, block_cols] = scaled.astype(jnp.bfloat16)
+        for t in range(2):
+            tile = scaled[:, t * 128 : (t + 1) * 128]
+            flipped[pl.ds(pl.multiple_of(n * 256 + t * 128, 128), 128), :] = tile.T.astype(jnp.bfloat16)
+        return loss + jnp.sum(diff * diff)
+
+    loss = jnp.float32(0.0)
+    for half in (0, 1):
+        for slot in (1, 2):
+            ref = parts.at[slot, :, side(half)]
+            remote(ref, ref, osend.at[0], orecv.at[slot * 2 + half], at(z, x, 1 - core)).wait_recv()
+
+        @pl.when(core == kept)
+        def _():
+            for zq in (0, 1):
+
+                @pl.when(is_own(zq))
+                def _():
+                    keep(zq, half).wait()
+
+        @pl.when(core != kept)
+        def _():
+            ref = parts.at[0, :, side(half)]
+            remote(ref, ref, osend.at[0], orecv.at[half], at(z, x, 1 - core)).wait_recv()
+
+        loss = lax.fori_loop(half * 7, half * 7 + 7, compare, loss)
+        for i in range(1, 8):
+            flip(half, i).start()
+
+        @pl.when(tp // 8 == half)
+        def _():
+            own_flip.start()
+
+        @pl.when(tp // 8 != half)
+        def _():
+            flip(half, 0).start()
+
+    norm_here.wait()
+    for i in range(4):
+        norm_wait(z + i, other)
+    norm_half(core).start()
 
     back = [jnp.dot(delta[...], proj_ref[k], preferred_element_type=jnp.float32) for k in range(4)]
     dots = jnp.zeros((ROWS, 1), jnp.float32)
@@ -698,20 +788,43 @@
         far = total_in.at[group(i)]
         remote(far, far, tsend.at[0], trecv.at[group(i)], {"dp": group(i)}).wait_recv()
     total_in[dp] = total[...]
-    stat_ref[...] = jnp.sum(total_in[...], axis=0)
+    whole = jnp.sum(total_in[...], axis=0)
+    stat_ref[:8, :] = whole[:8, :]
+    stat_ref[8:, :] = whole[8:, :] / terms
 
     for zq in (0, 1):
         swap(zq).wait_send()
-        for s in (0, 1):
-
-            @pl.when((2 * core + zq != z) | (core != s))
+        for half in (0, 1):
+
+            @pl.when(is_far(zq))
             def _():
-                give(zq, s).wait_send()
+                for s in (0, 1):
+                    pass_on(zq, s, half).wait_send()
+
+            @pl.when(is_near(zq))
+            def _():
+                for s in (0, 1):
+                    give(zq, s, half).wait_send()
+
+            @pl.when(is_own(zq))
+            def _():
+                hand_over(zq, half).wait_send()
+
+                @pl.when(core != kept)
+                def _():
+                    keep(zq, half).wait()
 
     for copy in norm_going + [norm_on(i) for i in (1, 2, 3)] + [norm_half(core)]:
         copy.wait_send()
+    for half in (0, 1):
+        for i in range(1, 8):
+            flip(half, i).wait_send()
+
+        @pl.when(tp // 8 != half)
+        def _():
+            flip(half, 0).wait_send()
+
     for i in range(1, 16):
-        flip(i).wait_send()
         tell(i).wait_send()
     for i in range(1, 8):
         hand(i).wait_send()
@@ -723,7 +836,7 @@
     own_column.wait()
 
 
-def student(key_len, row_len, factor, qkv, w_out, hidden, proj, rows, gain):
+def student(lengths, loss_scale, qkv, w_out, hidden, proj, rows, gain):
     vmem = pl.BlockSpec(memory_space=pltpu.VMEM)
     smem = pl.BlockSpec(memory_space=pltpu.SMEM)
     hbm = pl.BlockSpec(memory_space=pltpu.HBM)
@@ -735,7 +848,7 @@
             jax.ShapeDtypeStruct((PROJ, DS), jnp.bfloat16),
             jax.ShapeDtypeStruct((16, 128), jnp.float32),
         ),
-        in_specs=[smem, smem, smem, vmem, hbm, hbm, hbm, vmem, vmem],
+        in_specs=[smem, smem, vmem, hbm, hbm, hbm, vmem, vmem],
         out_specs=(vmem, vmem, vmem),
         scratch_shapes=[
             pltpu.VMEM((4, 256, HW), jnp.bfloat16),
@@ -746,7 +859,8 @@
             pltpu.VMEM((4, 2, 256, 256), jnp.bfloat16),
             pltpu.VMEM((2, 2, 256, 256), jnp.bfloat16),
             pltpu.VMEM((2, 256, HW), jnp.bfloat16),
-            pltpu.VMEM((4, ROWS, HW), jnp.bfloat16),
+            pltpu.VMEM((3, ROWS, HW), jnp.bfloat16),
+            pltpu.VMEM((ROWS, HW), jnp.bfloat16),
             pltpu.VMEM((ROWS, HW), jnp.float32),
             pltpu.VMEM((ROWS, HW), jnp.bfloat16),
             pltpu.VMEM((HW, ROWS), jnp.bfloat16),
@@ -759,35 +873,49 @@
             pltpu.VMEM((8, PROJ, 128), jnp.bfloat16),
             pltpu.VMEM((PROJ, 128), jnp.bfloat16),
         ]
-        + [pltpu.SemaphoreType.DMA((n,)) for n in (2, 2, 4, 4, 8, 9, 15, 16, 15, 16, 7, 8, 7, 8, 7, 8, 6)],
+        + [pltpu.SemaphoreType.DMA((n,)) for n in (2, 2, 8, 6, 2, 8, 9, 16, 16, 15, 16, 7, 8, 7, 8, 7, 8, 6)],
         compiler_params=pltpu.CompilerParams(
             collective_id=1, has_side_effects=True, vmem_limit_bytes=56 * MIB
         ),
-    )(key_len, row_len, factor, qkv, w_out, hidden, proj, rows, gain)
+    )(lengths, loss_scale, qkv, w_out, hidden, proj, rows, gain)
+
+
+def finish_kernel(grad_in, proj_in, stat_in, grad_ref, proj_ref, gain_ref, loss_ref):
+    grad_ref[...] = grad_in[...]
+    proj_ref[...] = proj_in[...]
+    gain_ref[...] = stat_in[:8, :]
+    loss_ref[...] = stat_in[8:9, :1]
+
+
+def finish(grad, proj, stat):
+    return pl.pallas_call(
+        finish_kernel,
+        name="finish",
+        out_shape=(
+            jax.ShapeDtypeStruct(grad.shape, grad.dtype),
+            jax.ShapeDtypeStruct(proj.shape, proj.dtype),
+            jax.ShapeDtypeStruct((8, 128), jnp.float32),
+            jax.ShapeDtypeStruct((1, 1), jnp.float32),
+        ),
+    )(grad, proj, stat)
 
 
 def shards(
     hidden_in, norm_gain, w_qkv, w_out, lengths, student_in, student_gain, proj_weight, loss_scale
 ):
-    tp = lax.axis_index("tp")
-    group = lax.axis_index("dp")
-    count = jnp.sum(lengths).astype(jnp.float32)
-    factor = 2.0 * loss_scale / (count * HW)
-    gain = student_gain.reshape(1, DS)
-
     qkv, w_out_all, proj_all = project(hidden_in, norm_gain.reshape(1, D), w_qkv, w_out, proj_weight)
     row_grad, proj_grad, stat = student(
-        lax.dynamic_slice_in_dim(lengths, group * SEQS + tp % 2, 1),
-        lax.dynamic_slice_in_dim(lengths, group * SEQS + tp // 8, 1),
-        factor,
+        lengths,
+        loss_scale,
         qkv,
         w_out_all,
         hidden_in,
         proj_all.reshape(4, HW, 256),
         student_in,
-        gain,
+        student_gain.reshape(1, DS),
     )
-    return row_grad, proj_grad, stat[:8].reshape(DS), stat[8, 0] / (count * HW)
+    row_grad, proj_grad, gain, loss = finish(row_grad, proj_grad, stat)
+    return row_grad, proj_grad, gain.reshape(DS), loss.reshape(())
 
 
 def solution(mesh):

time: 257 us -> 217 us (0.84)
  the two profiles are of different devices: /device:TPU:1 before, /device:TPU:104 now
where the time goes in v4:
time: 217 us
  Pallas kernels  216 us (100%)
    pallas_call x1, Pallas kernels, project(): pl.pallas_call(project_kernel, name='project', out_shape=(jax.ShapeDtypeS...  119 us
    pallas_call x1, Pallas kernels, student(): pl.pallas_call(student_kernel, name='student', out_shape=(jax.ShapeDtypeS...  95 us

profile of v4, /device:TPU:104, one launch (start us, length us, event | category | flops | bytes accessed | tf_op | source)
XLA Modules:
  0.0 217.3 jit_solution(5004057416041938116)
XLA Ops:
  1.3 119.0 %project.1 = (bf16[6,1024,256]{2,1,0:T(8,128)(2,1)}, bf16[4,256,3584]{2,1,0:T(8,128)(2,1)}, bf16[4,8,2,224,256]{4,3,2,1,0:T(8,128)(2,1)}) custom-call(bf16[128,7168]{1,0:T(8,128)(2,1)} %hid_hbm.1, f32[1,7168]{1,0:T(1,128)} %bitcast.6, bf16[3,7168,256]{2,1,0:T(8,128)(2,1)} %w_hbm.1, bf16[256,3584]{1,0:T(8,128)(2,1)} %wout_hbm.1, bf16[224,1024]{1,0:T(8,128)(2,1)} %proj_hbm.1), custom_call_target="tpu_custom_call" | custom-call | tf_op jit(solution)/shard_map/project/pallas_call | solution.py:348
  120.3 95.0 %student.1 = (bf16[128,1024]{1,0:T(8,128)(2,1)}, bf16[224,1024]{1,0:T(8,128)(2,1)}, f32[16,128]{1,0:T(8,128)}) custom-call(s32[16]{0:T(128)} %len_ref.1, f32[1]{0:T(128)S(6)} %copy.13.scale_ref, bf16[6,1024,256]{2,1,0:T(8,128)(2,1)} %get-tuple-element.14.qkv_ref, bf16[4,256,3584]{2,1,0:T(8,128)(2,1)} %get-tuple-element.15.wout_hbm, ...), custom_call_target="tpu_custom_call" | custom-call | tf_op jit(solution)/shard_map/student/pallas_call | solution.py:843
  215.3 2.0 finish.1

commit v5 on v4

--- a/solution.py
+++ b/solution.py
@@ -17,7 +17,7 @@
 DS = 1024
 PROJ = 224
 ROWS = 128
-FIRST = 80
+FIRST = (80, 64)
 MESH = pl.DeviceIdType.MESH
 MIB = 1 << 20
 
@@ -51,10 +51,11 @@
     return rows * lax.rsqrt(jnp.mean(rows * rows, axis=-1, keepdims=True) + 1e-06) * gain
 
 
-def greet(devices):
+def greet(devices, meanwhile):
     barrier = pltpu.get_barrier_semaphore()
     for device in devices:
         pl.semaphore_signal(barrier, 1, device_id=device, device_id_type=MESH)
+    meanwhile()
     pl.semaphore_wait(barrier, len(devices))
 
 
@@ -88,8 +89,18 @@
     step = jnp.where(ahead, 1, -1)
     near = (z + step + 4) % 4
     onward = (z - step + 4) % 4
-    via = jnp.where(ahead, 1, 0)
     far = (z + 2) % 4
+
+    def norm(start, size):
+        def one(i, carry):
+            block = pl.ds(pl.multiple_of(start + i * 16, 16), 16)
+            values = x_ref[block, :].astype(jnp.float32)
+            centred = values - jnp.mean(values, axis=-1, keepdims=True)
+            spread = jnp.mean(centred * centred, axis=-1, keepdims=True)
+            normed[block, :] = (centred * lax.rsqrt(spread + 1e-05) * gain_ref[...]).astype(jnp.bfloat16)
+            return carry
+
+        lax.fori_loop(0, size // 16, one, 0)
 
     greet(
         [at(z, x, 1 - core)]
@@ -97,7 +108,8 @@
         + [at(z, other, c) for c in (0, 1)]
         + [across(z, x, c) for c in (0, 1)]
         + [at(far, x, core)]
-        + [beside(z, x, core, i) for i in (1, 2, 3)]
+        + [beside(z, x, core, i) for i in (1, 2, 3)],
+        lambda: norm(min(FIRST), ROWS - min(FIRST)),
     )
 
     y = lax.axis_index("dp") % 4
@@ -111,19 +123,21 @@
     quarter = proj_hbm.at[:, pl.ds(pl.multiple_of(y * 256, 256), 256)]
     quarter_here = pltpu.make_async_copy(quarter, held(z, x), local.at[6])
     quarter_going = [
-        remote(quarter, held(z, x), psend.at[i], held_sem(z, x), at(zz, xx, core))
-        for i, (zz, xx) in enumerate(((z + 1, x), (z + 3, x), (z + 2, x), (z, other)))
+        remote(quarter, held(z, x), psend.at[i], held_sem(z, x), device)
+        for i, device in enumerate(
+            (at(z + 1, x, core), at(z + 3, x, core), at(z + 2, x, core), across(z, x, core))
+        )
     ]
     for copy in [quarter_here] + quarter_going:
         copy.start()
 
     def quarter_wait(chip_z, chip_x):
         ref = held(chip_z, chip_x)
-        remote(ref, ref, psend.at[0], held_sem(chip_z, chip_x), at(z, other, core)).wait_recv()
+        remote(ref, ref, psend.at[0], held_sem(chip_z, chip_x), across(z, x, core)).wait_recv()
 
     def quarter_on(i):
         ref = held(z + i, x)
-        return remote(ref, ref, psend.at[3 + i], held_sem(z + i, x), at(z, other, core))
+        return remote(ref, ref, psend.at[3 + i], held_sem(z + i, x), across(z, x, core))
 
     def along(i):
         ref = proj_all.at[y, :, core]
@@ -144,13 +158,13 @@
         remote(wout_hbm, wout_all.at[slot], wsend.at[5], wrecv.at[5 + core], across(z, x, 1)),
     ]
     proj_own = pltpu.make_async_copy(wout_hbm, wout_all.at[slot], local.at[3])
-    for copy in w_own + w_out_going + proj_going + [proj_own]:
+    for copy in w_own + w_out_going + proj_going[:1] + [proj_own]:
         copy.start()
 
     def part(chunk_z, chunk_x, s, cls):
         chunk = (chunk_z % 2) * 2 + chunk_x
-        start, size = ((0, FIRST), (FIRST, ROWS - FIRST))[cls]
-        return rows.at[chunk, pl.ds(pl.multiple_of(s * ROWS + start, 16), size)]
+        start, size = ((0, FIRST[s]), (FIRST[s], ROWS - FIRST[s]))[cls]
+        return rows.at[chunk, pl.ds(s * ROWS + start, size)]
 
     def sem(chunk_z, chunk_x, s, cls):
         return recv.at[((chunk_z % 2) * 2 + chunk_x) * 4 + s * 2 + cls]
@@ -163,22 +177,11 @@
         ref = part(chunk_z, chunk_x, s, cls)
         return remote(ref, ref, send.at[index], sem(chunk_z, chunk_x, s, cls), device)
 
-    def norm(start, size):
-        def one(i, carry):
-            block = pl.ds(pl.multiple_of(start + i * 16, 16), 16)
-            values = x_ref[block, :].astype(jnp.float32)
-            centred = values - jnp.mean(values, axis=-1, keepdims=True)
-            spread = jnp.mean(centred * centred, axis=-1, keepdims=True)
-            normed[block, :] = (centred * lax.rsqrt(spread + 1e-05) * gain_ref[...]).astype(jnp.bfloat16)
-            return carry
-
-        lax.fori_loop(0, size // 16, one, 0)
-
-    def own_copies(cls):
-        start, size = ((0, FIRST), (FIRST, ROWS - FIRST))[cls]
+    def own_copies(cls, s):
+        start, size = ((0, FIRST[s]), (FIRST[s], ROWS - FIRST[s]))[cls]
         src = normed.at[pl.ds(start, size)]
-        dst = part(z, x, core, cls)
-        got = sem(z, x, core, cls)
+        dst = part(z, x, s, cls)
+        got = sem(z, x, s, cls)
         base = cls * 4
         return (
             [
@@ -190,43 +193,63 @@
             pltpu.make_async_copy(src, dst, local.at[4 + cls]),
         )
 
-    for cls, (start, size) in ((1, (FIRST, ROWS - FIRST)), (0, (0, FIRST))):
-        norm(start, size)
-        away, sibling, here = own_copies(cls)
-        for copy in away:
-            copy.start()
-
-        @pl.when(core == kept)
-        def _():
-            here.start()
-
-        @pl.when(core != kept)
-        def _():
-            sibling.start()
-
-    def multiply(chunk_z, chunk_x):
+    for cls in (1, 0):
+        if cls == 0:
+            norm(0, min(FIRST))
+        for s in (0, 1):
+
+            @pl.when(core == s)
+            def _():
+                away, sibling, here = own_copies(cls, s)
+                for copy in away:
+                    copy.start()
+
+                @pl.when(core == kept)
+                def _():
+                    here.start()
+
+                @pl.when(core != kept)
+                def _():
+                    sibling.start()
+
+    def multiply(chunk_z, chunk_x, start=0, size=2 * ROWS):
         chunk = (chunk_z % 2) * 2 + chunk_x
 
         def one(n, carry):
-            out = jnp.dot(rows[chunk], w[n % 2, n // 2], preferred_element_type=jnp.float32)
-            qkv_ref[n, pl.ds(pl.multiple_of(chunk * 256, 256), 256), :] = out.astype(jnp.bfloat16)
+            out = jnp.dot(
+                rows[chunk, start : start + size], w[n % 2, n // 2], preferred_element_type=jnp.float32
+            )
+            qkv_ref[n, pl.ds(pl.multiple_of(chunk * 256 + start, 128), size), :] = out.astype(jnp.bfloat16)
             return carry
 
         lax.fori_loop(0, 6, one, 0)
+
+    source = rel < 2
 
     for i in (1, 3, 2):
         quarter_wait(z + i, x)
         quarter_on(i).start()
-
-    source = rel < 2
+    for copy in proj_going[1:]:
+        copy.start()
 
     fx = []
     for s in (0, 1):
         arrived(near, x, s, 1)
         fx.append(forward(near, x, s, 1, 8 + s, at(z, other, core)))
         fx[-1].start()
-    on_b = forward(near, x, via, 1, 10, at(onward, x, core))
-    on_b.start()
+    def pass_on(chunk_x, cls, index):
+        return [
+            (ahead == bool(s), forward(near, chunk_x, s, cls, index, at(onward, x, core))) for s in (0, 1)
+        ]
+
+    def begin(pairs):
+        for mine, copy in pairs:
+
+            @pl.when(mine)
+            def _():
+                copy.start()
+
+    begin(pass_on(x, 1, 10))
 
     for copy in w_own:
         copy.wait()
@@ -236,8 +259,16 @@
     @pl.when(source)
     def _():
         for cls in (0, 1):
-            arrived(z, x, 1 - core, cls)
-            own_copies(cls)[2].wait()
+            for s in (0, 1):
+
+                @pl.when(core != s)
+                def _():
+                    arrived(z, x, s, cls)
+
+                @pl.when(core == s)
+                def _():
+                    own_copies(cls, s)[2].wait()
+
         multiply(z, x)
 
     quarter_here.wait()
@@ -248,8 +279,7 @@
 
     for s in (0, 1):
         arrived(near, x, s, 0)
-    on_a = forward(near, x, via, 0, 11, at(onward, x, core))
-    on_a.start()
+    begin(pass_on(x, 0, 11))
 
     def spread():
         return [
@@ -281,21 +311,20 @@
 
     for s in (0, 1):
         arrived(near, other, s, 0)
-    on_p = forward(near, other, via, 0, 16, at(onward, x, core))
-    on_p.start()
+    begin(pass_on(other, 0, 16))
 
     @pl.when(source)
     def _():
         multiply(near, x)
-
-    for s in (0, 1):
-        arrived(near, other, s, 1)
-    multiply(near, other)
 
     for i in (1, 2, 3):
         ref = proj_all.at[(y + i) % 4, :, core]
         remote(ref, ref, ysend.at[0], yrecv.at[(y + i) % 4], at(z, x, 1 - core)).wait_recv()
     halves(core).start()
+
+    for s in (0, 1):
+        arrived(near, other, s, 1)
+    multiply(near, other)
 
     @pl.when(jnp.logical_not(source))
     def _():
@@ -305,19 +334,28 @@
         for s in (0, 1):
             arrived(far, other, s, 0)
             arrived(far, other, s, 1)
-        multiply(far, other)
+            multiply(far, other, s * ROWS, ROWS)
 
     for cls in (0, 1):
-        away, sibling, here = own_copies(cls)
-        for copy in away:
+        for s in (0, 1):
+
+            @pl.when(core == s)
+            def _():
+                away, sibling, here = own_copies(cls, s)
+                for copy in away:
+                    copy.wait_send()
+
+                @pl.when(core != kept)
+                def _():
+                    sibling.wait_send()
+
+    for copy in fx:
+        copy.wait_send()
+    for mine, copy in pass_on(x, 1, 10) + pass_on(x, 0, 11) + pass_on(other, 0, 16):
+
+        @pl.when(mine)
+        def _():
             copy.wait_send()
-
-        @pl.when(core != kept)
-        def _():
-            sibling.wait_send()
-
-    for copy in fx + [on_b, on_a, on_p]:
-        copy.wait_send()
 
     @pl.when(source)
     def _():
@@ -448,38 +486,9 @@
     def group(i):
         return (dp + i) % 8
 
-    greet([{"tp": mate(i)} for i in range(1, 16)] + [{"dp": group(i)} for i in range(1, 8)])
-
     rows = student_ref[...].astype(jnp.float32)
     scale = lax.rsqrt(jnp.mean(rows * rows, axis=-1, keepdims=True) + 1e-06)
     normed[...] = (rows * scale * gain_ref[...]).astype(jnp.bfloat16)
-
-    def block(chip_z, chip_x, c):
-        chip = (chip_z % 4) * 2 + chip_x
-        return norm_ref.at[pl.ds(pl.multiple_of((c * 8 + chip) * ROWS, 128), ROWS)]
-
-    def block_sem(chip_z, chip_x):
-        return nrecv.at[(chip_z % 4) * 2 + chip_x]
-
-    norm_here = pltpu.make_async_copy(normed, block(z, x, core), local.at[3])
-    norm_going = [
-        remote(normed, block(z, x, core), nsend.at[i], block_sem(z, x), at(zz, xx, core))
-        for i, (zz, xx) in enumerate(((z + 1, x), (z + 3, x), (z + 2, x), (z, other)))
-    ]
-    for copy in [norm_here] + norm_going[:3]:
-        copy.start()
-
-    def norm_wait(chip_z, chip_x):
-        ref = block(chip_z, chip_x, core)
-        remote(ref, ref, nsend.at[0], block_sem(chip_z, chip_x), at(z, other, core)).wait_recv()
-
-    def norm_on(i):
-        ref = block(z + i, x, core)
-        return remote(ref, ref, nsend.at[3 + i], block_sem(z + i, x), at(z, other, core))
-
-    def norm_half(c):
-        ref = norm_ref.at[pl.ds(pl.multiple_of(c * LEN, 128), LEN)]
-        return remote(ref, ref, nsend.at[7], nrecv.at[8], at(z, x, 1 - core))
 
     def attend(chunk, keys, zq, mine):
         start = pl.multiple_of(chunk * 256, 256)
@@ -508,6 +517,37 @@
     def swap(zq):
         return remote(ctx.at[zq * 2], ctx_in.at[zq], send.at[zq], recv.at[zq], at(z, other, core))
 
+    greet(
+        [{"tp": mate(i)} for i in range(1, 16)] + [{"dp": group(i)} for i in range(1, 8)],
+        lambda: attend(other, 512, 0, 0),
+    )
+    swap(0).start()
+
+    def block(chip_z, chip_x, c):
+        chip = (chip_z % 4) * 2 + chip_x
+        return norm_ref.at[pl.ds(pl.multiple_of((c * 8 + chip) * ROWS, 128), ROWS)]
+
+    def block_sem(chip_z, chip_x):
+        return nrecv.at[(chip_z % 4) * 2 + chip_x]
+
+    norm_here = pltpu.make_async_copy(normed, block(z, x, core), local.at[3])
+    norm_going = [
+        remote(normed, block(z, x, core), nsend.at[i], block_sem(z, x), at(zz, xx, core))
+        for i, (zz, xx) in enumerate(((z + 1, x), (z + 3, x), (z + 2, x), (z, other)))
+    ]
+
+    def norm_wait(chip_z, chip_x):
+        ref = block(chip_z, chip_x, core)
+        remote(ref, ref, nsend.at[0], block_sem(chip_z, chip_x), at(z, other, core)).wait_recv()
+
+    def norm_on(i):
+        ref = block(z + i, x, core)
+        return remote(ref, ref, nsend.at[3 + i], block_sem(z + i, x), at(z, other, core))
+
+    def norm_half(c):
+        ref = norm_ref.at[pl.ds(pl.multiple_of(c * LEN, 128), LEN)]
+        return remote(ref, ref, nsend.at[7], nrecv.at[8], at(z, x, 1 - core))
+
     def side(half):
         return pl.ds(half * HALF, HALF)
 
@@ -604,18 +644,16 @@
             lax.fori_loop(0, ROWS // 16, one, 0)
             give(zq, via, half).start()
 
-    attend(other, 512, 0, 0)
-    swap(0).start()
+    for copy in [norm_here] + norm_going[:3]:
+        copy.start()
+    attend(2 + other, 1024, 1, 0)
+    swap(1).start()
     attend(x, 512, 0, 1)
     fetch_wout.wait()
     swap(0).wait_recv()
     for half in (0, 1):
         project_out(0, half)
-    attend(2 + other, 1024, 1, 0)
-    swap(1).start()
     attend(2 + x, 1024, 1, 1)
-    for half in (0, 1):
-        join(0, half)
     swap(1).wait_recv()
     for half in (0, 1):
         project_out(1, half)
@@ -623,8 +661,7 @@
     for i in (1, 3, 2):
         norm_wait(z + i, x)
         norm_on(i).start()
-    for half in (0, 1):
-        join(1, half)
+    join(0, 0)
 
     fetch_proj.wait()
 
@@ -642,8 +679,10 @@
         return carry
 
     lax.fori_loop(0, HW // 512, map_rows, 0)
+    join(0, 1)
+    for half in (0, 1):
+        join(1, half)
     fetch_hid.wait()
-
     position = (tp % 8) * ROWS + lax.broadcasted_iota(jnp.int32, (ROWS, 1), 0)
     valid = position < len_ref[dp * SEQS + kept]
     lane = pl.ds(pl.multiple_of((core * 8 + z * 2 + x) * ROWS, 128), ROWS)
@@ -740,17 +779,19 @@
         remote(got, got, dsend.at[0], drecv.at[far], {"tp": far}).wait_recv()
     own_flip.wait()
 
-    def hand(i):
-        return remote(piece.at[group(i)], piece_in.at[dp], gsend.at[i - 1], grecv.at[dp], {"dp": group(i)})
+    def hand(g):
+        return remote(piece.at[g], piece_in.at[dp], gsend.at[g], grecv.at[dp], {"dp": g})
 
     for k in range(4):
         out = jnp.dot(
             flipped_in[...], norm_ref[:, k * 256 : (k + 1) * 256], preferred_element_type=jnp.float32
         ).astype(jnp.bfloat16)
-        piece[2 * k] = out[:, :128]
-        piece[2 * k + 1] = out[:, 128:]
-    for i in range(1, 8):
-        hand(i).start()
+        for g in (2 * k, 2 * k + 1):
+            piece[g] = out[:, (g % 2) * 128 : (g % 2 + 1) * 128]
+
+            @pl.when(dp != g)
+            def _():
+                hand(g).start()
 
     for i in range(1, 16):
         far = stat_in.at[mate(i)]
@@ -826,8 +867,13 @@
 
     for i in range(1, 16):
         tell(i).wait_send()
+    for g in range(8):
+
+        @pl.when(dp != g)
+        def _():
+            hand(g).wait_send()
+
     for i in range(1, 8):
-        hand(i).wait_send()
         tell_groups(i).wait_send()
     for i in range(1, 8):
         far = column(group(i))
@@ -873,7 +919,7 @@
             pltpu.VMEM((8, PROJ, 128), jnp.bfloat16),
             pltpu.VMEM((PROJ, 128), jnp.bfloat16),
         ]
-        + [pltpu.SemaphoreType.DMA((n,)) for n in (2, 2, 8, 6, 2, 8, 9, 16, 16, 15, 16, 7, 8, 7, 8, 7, 8, 6)],
+        + [pltpu.SemaphoreType.DMA((n,)) for n in (2, 2, 8, 6, 2, 8, 9, 16, 16, 15, 16, 7, 8, 8, 8, 7, 8, 6)],
         compiler_params=pltpu.CompilerParams(
             collective_id=1, has_side_effects=True, vmem_limit_bytes=56 * MIB
         ),

time: 217 us -> 209 us (0.963)
  Pallas kernels: 216 us -> 207 us
    pallas_call x1, Pallas kernels: 95 us -> 88.9 us  [student(): pl.pallas_call(student_kernel, name='student', out_shape=(jax.ShapeDtypeS...]
    pallas_call x1, Pallas kernels: 119 us -> 116 us  [project(): pl.pallas_call(project_kernel, name='project', out_shape=(jax.ShapeDtypeS...]
where the time goes in v5:
time: 209 us; the launch traced here: 208 us
  Pallas kernels  207 us (99%)
    pallas_call x1, Pallas kernels, project(): pl.pallas_call(project_kernel, name='project', out_shape=(jax.ShapeDtypeS...  116 us
    pallas_call x1, Pallas kernels, student(): pl.pallas_call(student_kernel, name='student', out_shape=(jax.ShapeDtypeS...  88.9 us

profile of v5, /device:TPU:104, one launch (start us, length us, event | category | flops | bytes accessed | tf_op | source)
XLA Modules:
  0.0 208.3 jit_solution(10276683335312237194)
XLA Ops:
  1.3 116.1 %project.1 = (bf16[6,1024,256]{2,1,0:T(8,128)(2,1)}, bf16[4,256,3584]{2,1,0:T(8,128)(2,1)}, bf16[4,8,2,224,256]{4,3,2,1,0:T(8,128)(2,1)}) custom-call(bf16[128,7168]{1,0:T(8,128)(2,1)} %hid_hbm.1, f32[1,7168]{1,0:T(1,128)} %bitcast.6, bf16[3,7168,256]{2,1,0:T(8,128)(2,1)} %w_hbm.1, bf16[256,3584]{1,0:T(8,128)(2,1)} %wout_hbm.1, bf16[224,1024]{1,0:T(8,128)(2,1)} %proj_hbm.1), custom_call_target="tpu_custom_call" | custom-call | tf_op jit(solution)/shard_map/project/pallas_call | solution.py:386
  117.4 88.9 %student.1 = (bf16[128,1024]{1,0:T(8,128)(2,1)}, bf16[224,1024]{1,0:T(8,128)(2,1)}, f32[16,128]{1,0:T(8,128)}) custom-call(s32[16]{0:T(128)} %len_ref.1, f32[1]{0:T(128)S(6)} %copy.13.scale_ref, bf16[6,1024,256]{2,1,0:T(8,128)(2,1)} %get-tuple-element.14.qkv_ref, bf16[4,256,3584]{2,1,0:T(8,128)(2,1)} %get-tuple-element.15.wout_hbm, ...), custom_call_target="tpu_custom_call" | custom-call | tf_op jit(solution)/shard_map/student/pallas_call | solution.py:889
  206.4 2.0 finish.1

commit v6 on v5

--- a/solution.py
+++ b/solution.py
@@ -10,7 +10,10 @@
 
 HEAD = 128
 HW = 3584
-HALF = HW // 2
+PARTS = 4
+WIDE = HW // PARTS
+TURN = (2, 1, 3, 0)
+EACH = 16 // PARTS
 LEN = 1024
 SEQS = 2
 D = 7168
@@ -193,24 +196,30 @@
             pltpu.make_async_copy(src, dst, local.at[4 + cls]),
         )
 
-    for cls in (1, 0):
-        if cls == 0:
-            norm(0, min(FIRST))
+    def send_own(cls, over_x, rest):
         for s in (0, 1):
 
             @pl.when(core == s)
             def _():
                 away, sibling, here = own_copies(cls, s)
-                for copy in away:
-                    copy.start()
-
-                @pl.when(core == kept)
-                def _():
-                    here.start()
-
-                @pl.when(core != kept)
-                def _():
-                    sibling.start()
+                if over_x:
+                    away[2].start()
+                if rest:
+                    for copy in away[:2]:
+                        copy.start()
+
+                    @pl.when(core == kept)
+                    def _():
+                        here.start()
+
+                    @pl.when(core != kept)
+                    def _():
+                        sibling.start()
+
+    send_own(1, False, True)
+    norm(0, min(FIRST))
+    send_own(0, True, True)
+    send_own(1, True, False)
 
     def multiply(chunk_z, chunk_x, start=0, size=2 * ROWS):
         chunk = (chunk_z % 2) * 2 + chunk_x
@@ -284,8 +293,7 @@
     def spread():
         return [
             forward(z, other, s, 0, 12 + s * 2 + i, at(zz, x, core))
-            for s in (0, 1)
-            for i, zz in enumerate((z + 1, z + 3))
+            for s, i, zz in ((0, 0, z + 1), (1, 1, z + 3), (1, 0, z + 1), (0, 1, z + 3))
         ]
 
     def crossing():
@@ -548,43 +556,43 @@
         ref = norm_ref.at[pl.ds(pl.multiple_of(c * LEN, 128), LEN)]
         return remote(ref, ref, nsend.at[7], nrecv.at[8], at(z, x, 1 - core))
 
-    def side(half):
-        return pl.ds(half * HALF, HALF)
-
-    def summand(zq, s, half):
-        return stage.at[zq, pl.ds(pl.multiple_of(s * ROWS, 16), ROWS), side(half)]
-
-    def give(zq, s, half):
+    def side(part):
+        return pl.ds(pl.multiple_of(jnp.int32(part * WIDE), 128), WIDE)
+
+    def summand(zq, s, part):
+        return stage.at[zq, pl.ds(pl.multiple_of(s * ROWS, 16), ROWS), side(part)]
+
+    def give(zq, s, part):
         slot = jnp.where(ahead, 2, 1)
         return remote(
-            summand(zq, s, half),
-            parts.at[slot, :, side(half)],
-            osend.at[zq * 4 + s * 2 + half],
-            orecv.at[slot * 2 + half],
+            summand(zq, s, part),
+            parts.at[slot, :, side(part)],
+            osend.at[(zq * 2 + s) * PARTS + part],
+            orecv.at[slot * PARTS + part],
             at(z + step + 4, x, s),
         )
 
-    def pass_on(zq, s, half):
+    def pass_on(zq, s, part):
         return remote(
-            summand(zq, s, half),
-            relay.at[:, side(half)],
-            osend.at[zq * 4 + s * 2 + half],
-            rrecv.at[half],
+            summand(zq, s, part),
+            relay.at[:, side(part)],
+            osend.at[(zq * 2 + s) * PARTS + part],
+            rrecv.at[part],
             at(z + (1 if s == 0 else 3), x, core),
         )
 
-    def hand_over(zq, half):
+    def hand_over(zq, part):
         return remote(
-            summand(zq, 1 - core, half),
-            parts.at[0, :, side(half)],
-            osend.at[zq * 4 + (1 - core) * 2 + half],
-            orecv.at[half],
+            summand(zq, 1 - core, part),
+            parts.at[0, :, side(part)],
+            osend.at[(zq * 2 + 1 - core) * PARTS + part],
+            orecv.at[part],
             at(z, x, 1 - core),
         )
 
-    def keep(zq, half):
+    def keep(zq, part):
         return pltpu.make_async_copy(
-            summand(zq, core, half), parts.at[0, :, side(half)], osend.at[zq * 4 + core * 2 + half]
+            summand(zq, core, part), parts.at[0, :, side(part)], osend.at[(zq * 2 + core) * PARTS + part]
         )
 
     def is_near(zq):
@@ -596,53 +604,48 @@
     def is_own(zq):
         return rel == zq
 
-    def project_out(zq, half):
-        def one(n, carry):
-            lanes = pl.ds(pl.multiple_of(half * HALF + n * 896, 128), 896)
-            out = jnp.zeros((256, 896), jnp.float32)
-            for k in (0, 1):
-                out += jnp.dot(
-                    ctx[zq * 2 + 1, k], wout_ref[x * 2 + k, :, lanes], preferred_element_type=jnp.float32
-                )
-                out += jnp.dot(
-                    ctx_in[zq, k], wout_ref[other * 2 + k, :, lanes], preferred_element_type=jnp.float32
-                )
-            stage[zq, :, lanes] = out.astype(jnp.bfloat16)
-            return carry
-
-        lax.fori_loop(0, HALF // 896, one, 0)
+    def project_out(zq, part):
+        out = jnp.zeros((256, WIDE), jnp.float32)
+        for k in (0, 1):
+            out += jnp.dot(
+                ctx[zq * 2 + 1, k], wout_ref[x * 2 + k, :, side(part)], preferred_element_type=jnp.float32
+            )
+            out += jnp.dot(
+                ctx_in[zq, k], wout_ref[other * 2 + k, :, side(part)], preferred_element_type=jnp.float32
+            )
+        stage[zq, :, side(part)] = out.astype(jnp.bfloat16)
 
         @pl.when(is_far(zq))
         def _():
             for s in (0, 1):
-                pass_on(zq, s, half).start()
+                pass_on(zq, s, part).start()
 
         @pl.when(is_near(zq))
         def _():
-            give(zq, 1 - via, half).start()
+            give(zq, 1 - via, part).start()
 
         @pl.when(is_own(zq))
         def _():
-            keep(zq, half).start()
-            hand_over(zq, half).start()
-
-    def join(zq, half):
+            keep(zq, part).start()
+            hand_over(zq, part).start()
+
+    def join(zq, part):
         @pl.when(is_near(zq))
         def _():
-            src = relay.at[:, side(half)]
-            remote(src, src, osend.at[0], rrecv.at[half], at(z, x, 1 - core)).wait_recv()
+            src = relay.at[:, side(part)]
+            remote(src, src, osend.at[0], rrecv.at[part], at(z, x, 1 - core)).wait_recv()
 
             def one(i, carry):
                 here = pl.ds(pl.multiple_of(via * ROWS + i * 16, 16), 16)
                 there = pl.ds(pl.multiple_of(i * 16, 16), 16)
-                both = stage[zq, here, side(half)].astype(jnp.float32) + relay[there, side(half)].astype(
+                both = stage[zq, here, side(part)].astype(jnp.float32) + relay[there, side(part)].astype(
                     jnp.float32
                 )
-                stage[zq, here, side(half)] = both.astype(jnp.bfloat16)
+                stage[zq, here, side(part)] = both.astype(jnp.bfloat16)
                 return carry
 
             lax.fori_loop(0, ROWS // 16, one, 0)
-            give(zq, via, half).start()
+            give(zq, via, part).start()
 
     for copy in [norm_here] + norm_going[:3]:
         copy.start()
@@ -651,17 +654,17 @@
     attend(x, 512, 0, 1)
     fetch_wout.wait()
     swap(0).wait_recv()
-    for half in (0, 1):
-        project_out(0, half)
+    for turn in TURN:
+        project_out(0, (2 * core + turn) % PARTS)
     attend(2 + x, 1024, 1, 1)
     swap(1).wait_recv()
-    for half in (0, 1):
-        project_out(1, half)
+    for turn in TURN:
+        project_out(1, (2 * core + 1 + turn) % PARTS)
     norm_going[3].start()
     for i in (1, 3, 2):
         norm_wait(z + i, x)
         norm_on(i).start()
-    join(0, 0)
+    join(0, (2 * core + TURN[0]) % PARTS)
 
     fetch_proj.wait()
 
@@ -679,21 +682,22 @@
         return carry
 
     lax.fori_loop(0, HW // 512, map_rows, 0)
-    join(0, 1)
-    for half in (0, 1):
-        join(1, half)
+    for turn in TURN[1:]:
+        join(0, (2 * core + turn) % PARTS)
+    for turn in TURN:
+        join(1, (2 * core + 1 + turn) % PARTS)
     fetch_hid.wait()
     position = (tp % 8) * ROWS + lax.broadcasted_iota(jnp.int32, (ROWS, 1), 0)
     valid = position < len_ref[dp * SEQS + kept]
     lane = pl.ds(pl.multiple_of((core * 8 + z * 2 + x) * ROWS, 128), ROWS)
 
-    def owner(half, i):
-        return half * 8 + (tp + i) % 8
-
-    def flip(half, i):
-        src = flipped.at[pl.ds(pl.multiple_of(owner(half, i) * PROJ, 16), PROJ)]
+    def owner(part, i):
+        return part * EACH + (tp + i) % EACH
+
+    def flip(part, i):
+        src = flipped.at[pl.ds(pl.multiple_of(owner(part, i) * PROJ, 16), PROJ)]
         return remote(
-            src, flipped_in.at[:, lane], dsend.at[half * 8 + i], drecv.at[tp], {"tp": owner(half, i)}
+            src, flipped_in.at[:, lane], dsend.at[part * EACH + i], drecv.at[tp], {"tp": owner(part, i)}
         )
 
     own_flip = pltpu.make_async_copy(
@@ -701,7 +705,7 @@
     )
 
     def compare(n, loss):
-        block_cols = pl.ds(pl.multiple_of(n * 256, 256), 256)
+        block_cols = pl.ds(pl.multiple_of(n * 128, 128), 128)
         mixed = parts[0, :, block_cols].astype(jnp.float32)
         for slot in (1, 2):
             mixed += parts[slot, :, block_cols].astype(jnp.float32)
@@ -709,16 +713,15 @@
         diff = jnp.where(valid, mapped[:, block_cols] - target.astype(jnp.float32), 0.0)
         scaled = diff * factor
         delta[:, block_cols] = scaled.astype(jnp.bfloat16)
-        for t in range(2):
-            tile = scaled[:, t * 128 : (t + 1) * 128]
-            flipped[pl.ds(pl.multiple_of(n * 256 + t * 128, 128), 128), :] = tile.T.astype(jnp.bfloat16)
-        return loss + jnp.sum(diff * diff)
-
-    loss = jnp.float32(0.0)
-    for half in (0, 1):
+        flipped[block_cols, :] = scaled.T.astype(jnp.bfloat16)
+        return loss + diff * diff
+
+    loss = jnp.zeros((ROWS, 128), jnp.float32)
+    for turn in TURN:
+        part = (z + turn) % PARTS
         for slot in (1, 2):
-            ref = parts.at[slot, :, side(half)]
-            remote(ref, ref, osend.at[0], orecv.at[slot * 2 + half], at(z, x, 1 - core)).wait_recv()
+            ref = parts.at[slot, :, side(part)]
+            remote(ref, ref, osend.at[0], orecv.at[slot * PARTS + part], at(z, x, 1 - core)).wait_recv()
 
         @pl.when(core == kept)
         def _():
@@ -726,24 +729,24 @@
 
                 @pl.when(is_own(zq))
                 def _():
-                    keep(zq, half).wait()
+                    keep(zq, part).wait()
 
         @pl.when(core != kept)
         def _():
-            ref = parts.at[0, :, side(half)]
-            remote(ref, ref, osend.at[0], orecv.at[half], at(z, x, 1 - core)).wait_recv()
-
-        loss = lax.fori_loop(half * 7, half * 7 + 7, compare, loss)
-        for i in range(1, 8):
-            flip(half, i).start()
-
-        @pl.when(tp // 8 == half)
+            ref = parts.at[0, :, side(part)]
+            remote(ref, ref, osend.at[0], orecv.at[part], at(z, x, 1 - core)).wait_recv()
+
+        loss = lax.fori_loop(part * (WIDE // 128), (part + 1) * (WIDE // 128), compare, loss)
+        for i in range(1, EACH):
+            flip(part, i).start()
+
+        @pl.when(tp // EACH == part)
         def _():
             own_flip.start()
 
-        @pl.when(tp // 8 != half)
-        def _():
-            flip(half, 0).start()
+        @pl.when(tp // EACH != part)
+        def _():
+            flip(part, 0).start()
 
     norm_here.wait()
     for i in range(4):
@@ -764,7 +767,7 @@
         part = jnp.sum(back[k] * (rows[:, cols] * scale), axis=0, keepdims=True)
         stat[2 * k : 2 * k + 1, :] = part[:, :128]
         stat[2 * k + 1 : 2 * k + 2, :] = part[:, 128:]
-    stat[8:16, :] = jnp.zeros((8, 128), jnp.float32) + loss
+    stat[8:16, :] = jnp.zeros((8, 128), jnp.float32) + jnp.sum(loss)
 
     def tell(i):
         return remote(stat, stat_in.at[tp], ssend.at[i - 1], srecv.at[tp], {"tp": mate(i)})
@@ -835,35 +838,35 @@
 
     for zq in (0, 1):
         swap(zq).wait_send()
-        for half in (0, 1):
+        for part in range(PARTS):
 
             @pl.when(is_far(zq))
             def _():
                 for s in (0, 1):
-                    pass_on(zq, s, half).wait_send()
+                    pass_on(zq, s, part).wait_send()
 
             @pl.when(is_near(zq))
             def _():
                 for s in (0, 1):
-                    give(zq, s, half).wait_send()
+                    give(zq, s, part).wait_send()
 
             @pl.when(is_own(zq))
             def _():
-                hand_over(zq, half).wait_send()
+                hand_over(zq, part).wait_send()
 
                 @pl.when(core != kept)
                 def _():
-                    keep(zq, half).wait()
+                    keep(zq, part).wait()
 
     for copy in norm_going + [norm_on(i) for i in (1, 2, 3)] + [norm_half(core)]:
         copy.wait_send()
-    for half in (0, 1):
-        for i in range(1, 8):
-            flip(half, i).wait_send()
-
-        @pl.when(tp // 8 != half)
-        def _():
-            flip(half, 0).wait_send()
+    for part in range(PARTS):
+        for i in range(1, EACH):
+            flip(part, i).wait_send()
+
+        @pl.when(tp // EACH != part)
+        def _():
+            flip(part, 0).wait_send()
 
     for i in range(1, 16):
         tell(i).wait_send()
@@ -919,7 +922,7 @@
             pltpu.VMEM((8, PROJ, 128), jnp.bfloat16),
             pltpu.VMEM((PROJ, 128), jnp.bfloat16),
         ]
-        + [pltpu.SemaphoreType.DMA((n,)) for n in (2, 2, 8, 6, 2, 8, 9, 16, 16, 15, 16, 7, 8, 8, 8, 7, 8, 6)],
+        + [pltpu.SemaphoreType.DMA((n,)) for n in (2, 2, 4 * PARTS, 3 * PARTS, PARTS, 8, 9, 16, 16, 15, 16, 7, 8, 8, 8, 7, 8, 6)],
         compiler_params=pltpu.CompilerParams(
             collective_id=1, has_side_effects=True, vmem_limit_bytes=56 * MIB
         ),

time: 209 us -> 206 us (0.986)
  the two profiles are of different devices: /device:TPU:104 before, /device:TPU:1 now
where the time goes in v6:
time: 206 us
  Pallas kernels  204 us (99%)
    pallas_call x1, Pallas kernels, project(): pl.pallas_call(project_kernel, name='project', out_shape=(jax.ShapeDtypeS...  120 us
    pallas_call x1, Pallas kernels, student(): pl.pallas_call(student_kernel, name='student', out_shape=(jax.ShapeDtypeS...  82.1 us

profile of v6, /device:TPU:1, one launch (start us, length us, event | category | flops | bytes accessed | tf_op | source)
XLA Modules:
  0.0 205.6 jit_solution(988744620985059612)
XLA Ops:
  1.3 120.3 %project.1 = (bf16[6,1024,256]{2,1,0:T(8,128)(2,1)}, bf16[4,256,3584]{2,1,0:T(8,128)(2,1)}, bf16[4,8,2,224,256]{4,3,2,1,0:T(8,128)(2,1)}) custom-call(bf16[128,7168]{1,0:T(8,128)(2,1)} %hid_hbm.1, f32[1,7168]{1,0:T(1,128)} %bitcast.6, bf16[3,7168,256]{2,1,0:T(8,128)(2,1)} %w_hbm.1, bf16[256,3584]{1,0:T(8,128)(2,1)} %wout_hbm.1, bf16[224,1024]{1,0:T(8,128)(2,1)} %proj_hbm.1), custom_call_target="tpu_custom_call" | custom-call | tf_op jit(solution)/shard_map/project/pallas_call | solution.py:394
  121.6 82.1 %student.1 = (bf16[128,1024]{1,0:T(8,128)(2,1)}, bf16[224,1024]{1,0:T(8,128)(2,1)}, f32[16,128]{1,0:T(8,128)}) custom-call(s32[16]{0:T(128)} %len_ref.1, f32[1]{0:T(128)S(6)} %copy.13.scale_ref, bf16[6,1024,256]{2,1,0:T(8,128)(2,1)} %get-tuple-element.14.qkv_ref, bf16[4,256,3584]{2,1,0:T(8,128)(2,1)} %get-tuple-element.15.wout_hbm, ...), custom_call_target="tpu_custom_call" | custom-call | tf_op jit(solution)/shard_map/student/pallas_call | solution.py:892
  203.7 2.0 finish.1

commit v7 on v6

--- a/solution.py
+++ b/solution.py
@@ -20,7 +20,7 @@
 DS = 1024
 PROJ = 224
 ROWS = 128
-FIRST = (80, 64)
+FIRST = (64, 64)
 MESH = pl.DeviceIdType.MESH
 MIB = 1 << 20
 
@@ -146,10 +146,6 @@
         ref = proj_all.at[y, :, core]
         return remote(ref, ref, ysend.at[i - 1], yrecv.at[y], beside(z, x, core, i))
 
-    def halves(c):
-        ref = proj_all.at[:, :, c]
-        return remote(ref, ref, ysend.at[3], yrecv.at[4], at(z, x, 1 - core))
-
     w_out_going = [
         remote(w_hbm.at[k], w.at[core, k], wsend.at[k], wrecv.at[k], at(z, x, 1 - core)) for k in range(3)
     ]
@@ -157,9 +153,10 @@
     slot = x * 2 + core
     proj_going = [
         remote(wout_hbm, wout_all.at[slot], wsend.at[3], wrecv.at[3 + core], at(z, x, 1 - core)),
-        remote(wout_hbm, wout_all.at[slot], wsend.at[4], wrecv.at[5 + core], across(z, x, 0)),
-        remote(wout_hbm, wout_all.at[slot], wsend.at[5], wrecv.at[5 + core], across(z, x, 1)),
+        remote(wout_hbm, wout_all.at[slot], wsend.at[4], wrecv.at[5 + core], across(z, x, core)),
     ]
+    far_slot = wout_all.at[other * 2 + core]
+    proj_on = remote(far_slot, far_slot, wsend.at[5], wrecv.at[5 + core], at(z, x, 1 - core))
     proj_own = pltpu.make_async_copy(wout_hbm, wout_all.at[slot], local.at[3])
     for copy in w_own + w_out_going + proj_going[:1] + [proj_own]:
         copy.start()
@@ -260,6 +257,7 @@
 
     begin(pass_on(x, 1, 10))
 
+
     for copy in w_own:
         copy.wait()
     for k in range(3):
@@ -325,10 +323,8 @@
     def _():
         multiply(near, x)
 
-    for i in (1, 2, 3):
-        ref = proj_all.at[(y + i) % 4, :, core]
-        remote(ref, ref, ysend.at[0], yrecv.at[(y + i) % 4], at(z, x, 1 - core)).wait_recv()
-    halves(core).start()
+    remote(far_slot, far_slot, wsend.at[4], wrecv.at[5 + core], across(z, x, core)).wait_recv()
+    proj_on.start()
 
     for s in (0, 1):
         arrived(near, other, s, 1)
@@ -375,17 +371,18 @@
         for copy in crossing():
             copy.wait_send()
 
-    for copy in w_out_going + proj_going + quarter_going + [quarter_on(i) for i in (1, 2, 3)]:
+    for copy in w_out_going + proj_going + [proj_on] + quarter_going + [quarter_on(i) for i in (1, 2, 3)]:
         copy.wait_send()
-    for copy in [along(i) for i in (1, 2, 3)] + [halves(core)]:
-        copy.wait_send()
-    halves(1 - core).wait_recv()
+    for i in (1, 2, 3):
+        along(i).wait_send()
+        ref = proj_all.at[(y + i) % 4, :, core]
+        remote(ref, ref, ysend.at[0], yrecv.at[(y + i) % 4], at(z, x, 1 - core)).wait_recv()
     proj_own.wait()
     remote(
         wout_hbm, wout_all.at[x * 2 + 1 - core], wsend.at[3], wrecv.at[3 + 1 - core], at(z, x, 1 - core)
     ).wait_recv()
-    for c in (0, 1):
-        remote(wout_hbm, wout_all.at[other * 2 + c], wsend.at[4], wrecv.at[5 + c], across(z, x, c)).wait_recv()
+    beyond = wout_all.at[other * 2 + 1 - core]
+    remote(beyond, beyond, wsend.at[5], wrecv.at[5 + 1 - core], at(z, x, 1 - core)).wait_recv()
 
 
 def project(hidden, gain, w_qkv, w_out, proj):
@@ -406,7 +403,7 @@
             pltpu.VMEM((4, 2 * ROWS, D), jnp.bfloat16),
             pltpu.VMEM((2, 3, D, 256), jnp.bfloat16),
         ]
-        + [pltpu.SemaphoreType.DMA((n,)) for n in (17, 16, 6, 7, 7, 8, 4, 5, 7)],
+        + [pltpu.SemaphoreType.DMA((n,)) for n in (17, 16, 6, 7, 7, 8, 3, 4, 7)],
         compiler_params=pltpu.CompilerParams(
             collective_id=0, has_side_effects=True, vmem_limit_bytes=60 * MIB
         ),
@@ -463,6 +460,9 @@
     grecv,
     asend,
     arecv,
+    plocal,
+    psend,
+    precv,
     local,
 ):
     z, x, core = place()
@@ -484,8 +484,21 @@
 
     fetch_wout = pltpu.make_async_copy(wout_hbm, wout_ref, local.at[0])
     fetch_hid = pltpu.make_async_copy(hid_hbm.at[:, pl.ds(0, HW)], hid_ref, local.at[1])
-    fetch_proj = pltpu.make_async_copy(proj_hbm, proj_ref, local.at[2])
-    for copy in (fetch_wout, fetch_hid, fetch_proj):
+
+    def proj_rows(chip, c):
+        return proj_ref.at[:, pl.ds(pl.multiple_of(chip * 2 * PROJ + c * PROJ, 16), PROJ)]
+
+    fetch_proj = [
+        pltpu.make_async_copy(proj_hbm.at[:, chip, core], proj_rows(chip, core), plocal.at[chip])
+        for chip in range(8)
+    ]
+    share_proj = [
+        remote(
+            proj_hbm.at[:, chip, core], proj_rows(chip, core), psend.at[chip], precv.at[chip], at(z, x, 1 - core)
+        )
+        for chip in range(8)
+    ]
+    for copy in [fetch_wout, fetch_hid] + fetch_proj:
         copy.start()
 
     def mate(i):
@@ -647,7 +660,7 @@
             lax.fori_loop(0, ROWS // 16, one, 0)
             give(zq, via, part).start()
 
-    for copy in [norm_here] + norm_going[:3]:
+    for copy in [norm_here] + norm_going[:3] + share_proj:
         copy.start()
     attend(2 + other, 1024, 1, 0)
     swap(1).start()
@@ -666,7 +679,10 @@
         norm_on(i).start()
     join(0, (2 * core + TURN[0]) % PARTS)
 
-    fetch_proj.wait()
+    for chip in range(8):
+        fetch_proj[chip].wait()
+        got = proj_rows(chip, 1 - core)
+        remote(got, got, psend.at[0], precv.at[chip], at(z, x, 1 - core)).wait_recv()
 
     def map_rows(n, carry):
         base = pl.multiple_of(n * 512, 512)
@@ -858,7 +874,7 @@
                 def _():
                     keep(zq, part).wait()
 
-    for copy in norm_going + [norm_on(i) for i in (1, 2, 3)] + [norm_half(core)]:
+    for copy in share_proj + norm_going + [norm_on(i) for i in (1, 2, 3)] + [norm_half(core)]:
         copy.wait_send()
     for part in range(PARTS):
         for i in range(1, EACH):
@@ -922,7 +938,7 @@
             pltpu.VMEM((8, PROJ, 128), jnp.bfloat16),
             pltpu.VMEM((PROJ, 128), jnp.bfloat16),
         ]
-        + [pltpu.SemaphoreType.DMA((n,)) for n in (2, 2, 4 * PARTS, 3 * PARTS, PARTS, 8, 9, 16, 16, 15, 16, 7, 8, 8, 8, 7, 8, 6)],
+        + [pltpu.SemaphoreType.DMA((n,)) for n in (2, 2, 4 * PARTS, 3 * PARTS, PARTS, 8, 9, 16, 16, 15, 16, 7, 8, 8, 8, 7, 8, 8, 8, 8, 6)],
         compiler_params=pltpu.CompilerParams(
             collective_id=1, has_side_effects=True, vmem_limit_bytes=56 * MIB
         ),
@@ -959,7 +975,7 @@
         qkv,
         w_out_all,
         hidden_in,
-        proj_all.reshape(4, HW, 256),
+        proj_all,
         student_in,
         student_gain.reshape(1, DS),
     )

time: 206 us -> 202 us (0.981)
  Pallas kernels: 204 us -> 200 us
    pallas_call x1, Pallas kernels: 120 us -> 118 us  [project(): pl.pallas_call(project_kernel, name='project', out_shape=(jax.ShapeDtypeS...]
where the time goes in v7:
time: 202 us; the launch traced here: 201 us
  Pallas kernels  200 us (99%)
    pallas_call x1, Pallas kernels, project(): pl.pallas_call(project_kernel, name='project', out_shape=(jax.ShapeDtypeS...  118 us
    pallas_call x1, Pallas kernels, student(): pl.pallas_call(student_kernel, name='student', out_shape=(jax.ShapeDtypeS...  80.1 us

profile of v7, /device:TPU:1, one launch (start us, length us, event | category | flops | bytes accessed | tf_op | source)
XLA Modules:
  0.0 201.0 jit_solution(11244037746393532869)
XLA Ops:
  1.3 117.6 %project.1 = (bf16[6,1024,256]{2,1,0:T(8,128)(2,1)}, bf16[4,256,3584]{2,1,0:T(8,128)(2,1)}, bf16[4,8,2,224,256]{4,3,2,1,0:T(8,128)(2,1)}) custom-call(bf16[128,7168]{1,0:T(8,128)(2,1)} %hid_hbm.1, f32[1,7168]{1,0:T(1,128)} %bitcast.4, bf16[3,7168,256]{2,1,0:T(8,128)(2,1)} %w_hbm.1, bf16[256,3584]{1,0:T(8,128)(2,1)} %wout_hbm.1, bf16[224,1024]{1,0:T(8,128)(2,1)} %proj_hbm.1), custom_call_target="tpu_custom_call" | custom-call | tf_op jit(solution)/shard_map/project/pallas_call | solution.py:391
  118.9 80.1 %student.1 = (bf16[128,1024]{1,0:T(8,128)(2,1)}, bf16[224,1024]{1,0:T(8,128)(2,1)}, f32[16,128]{1,0:T(8,128)}) custom-call(s32[16]{0:T(128)} %len_ref.1, f32[1]{0:T(128)S(6)} %copy.13.scale_ref, bf16[6,1024,256]{2,1,0:T(8,128)(2,1)} %get-tuple-element.14.qkv_ref, bf16[4,256,3584]{2,1,0:T(8,128)(2,1)} %get-tuple-element.15.wout_hbm, ...), custom_call_target="tpu_custom_call" | custom-call | tf_op jit(solution)/shard_map/student/pallas_call | solution.py:908
  199.0 2.0 finish.1

commit v8 on v7

--- a/solution.py
+++ b/solution.py
@@ -770,6 +770,27 @@
     norm_half(core).start()
 
     back = [jnp.dot(delta[...], proj_ref[k], preferred_element_type=jnp.float32) for k in range(4)]
+    norm_half(1 - core).wait_recv()
+    for i in range(1, 16):
+        far = mate(i)
+        got = flipped_in.at[:, pl.ds(pl.multiple_of(((far % 2) * 8 + far // 2) * ROWS, 128), ROWS)]
+        remote(got, got, dsend.at[0], drecv.at[far], {"tp": far}).wait_recv()
+    own_flip.wait()
+
+    def hand(g):
+        return remote(piece.at[g], piece_in.at[dp], gsend.at[g], grecv.at[dp], {"dp": g})
+
+    for k in range(4):
+        out = jnp.dot(
+            flipped_in[...], norm_ref[:, k * 256 : (k + 1) * 256], preferred_element_type=jnp.float32
+        ).astype(jnp.bfloat16)
+        for g in (2 * k, 2 * k + 1):
+            piece[g] = out[:, (g % 2) * 128 : (g % 2 + 1) * 128]
+
+            @pl.when(dp != g)
+            def _():
+                hand(g).start()
+
     dots = jnp.zeros((ROWS, 1), jnp.float32)
     for k in range(4):
         cols = slice(k * 256, (k + 1) * 256)
@@ -791,39 +812,6 @@
     for i in range(1, 16):
         tell(i).start()
 
-    norm_half(1 - core).wait_recv()
-    for i in range(1, 16):
-        far = mate(i)
-        got = flipped_in.at[:, pl.ds(pl.multiple_of(((far % 2) * 8 + far // 2) * ROWS, 128), ROWS)]
-        remote(got, got, dsend.at[0], drecv.at[far], {"tp": far}).wait_recv()
-    own_flip.wait()
-
-    def hand(g):
-        return remote(piece.at[g], piece_in.at[dp], gsend.at[g], grecv.at[dp], {"dp": g})
-
-    for k in range(4):
-        out = jnp.dot(
-            flipped_in[...], norm_ref[:, k * 256 : (k + 1) * 256], preferred_element_type=jnp.float32
-        ).astype(jnp.bfloat16)
-        for g in (2 * k, 2 * k + 1):
-            piece[g] = out[:, (g % 2) * 128 : (g % 2 + 1) * 128]
-
-            @pl.when(dp != g)
-            def _():
-                hand(g).start()
-
-    for i in range(1, 16):
-        far = stat_in.at[mate(i)]
-        remote(far, far, ssend.at[0], srecv.at[mate(i)], {"tp": mate(i)}).wait_recv()
-    stat_in[tp] = stat[...]
-    total[...] = jnp.sum(stat_in[...], axis=0)
-
-    def tell_groups(i):
-        return remote(total, total_in.at[dp], tsend.at[i - 1], trecv.at[dp], {"dp": group(i)})
-
-    for i in range(1, 8):
-        tell_groups(i).start()
-
     for i in range(1, 8):
         far = piece_in.at[group(i)]
         remote(far, far, gsend.at[0], grecv.at[group(i)], {"dp": group(i)}).wait_recv()
@@ -843,6 +831,18 @@
     own_column.start()
     for i in range(1, 8):
         publish(i).start()
+
+    for i in range(1, 16):
+        far = stat_in.at[mate(i)]
+        remote(far, far, ssend.at[0], srecv.at[mate(i)], {"tp": mate(i)}).wait_recv()
+    stat_in[tp] = stat[...]
+    total[...] = jnp.sum(stat_in[...], axis=0)
+
+    def tell_groups(i):
+        return remote(total, total_in.at[dp], tsend.at[i - 1], trecv.at[dp], {"dp": group(i)})
+
+    for i in range(1, 8):
+        tell_groups(i).start()
 
     for i in range(1, 8):
         far = total_in.at[group(i)]

time: 202 us -> 204 us (level)
  Pallas kernels: 200 us -> 203 us
    pallas_call x1, Pallas kernels: 80.1 us -> 83.4 us  [student(): pl.pallas_call(student_kernel, name='student', out_shape=(jax.ShapeDtypeS...]
where the time goes in v8:
time: 204 us
  Pallas kernels  203 us (100%)
    pallas_call x1, Pallas kernels, project(): pl.pallas_call(project_kernel, name='project', out_shape=(jax.ShapeDtypeS...  118 us
    pallas_call x1, Pallas kernels, student(): pl.pallas_call(student_kernel, name='student', out_shape=(jax.ShapeDtypeS...  83.4 us

profile of v8, /device:TPU:1, one launch (start us, length us, event | category | flops | bytes accessed | tf_op | source)
XLA Modules:
  0.0 204.3 jit_solution(4353811069625028960)
XLA Ops:
  1.3 117.6 %project.1 = (bf16[6,1024,256]{2,1,0:T(8,128)(2,1)}, bf16[4,256,3584]{2,1,0:T(8,128)(2,1)}, bf16[4,8,2,224,256]{4,3,2,1,0:T(8,128)(2,1)}) custom-call(bf16[128,7168]{1,0:T(8,128)(2,1)} %hid_hbm.1, f32[1,7168]{1,0:T(1,128)} %bitcast.4, bf16[3,7168,256]{2,1,0:T(8,128)(2,1)} %w_hbm.1, bf16[256,3584]{1,0:T(8,128)(2,1)} %wout_hbm.1, bf16[224,1024]{1,0:T(8,128)(2,1)} %proj_hbm.1), custom_call_target="tpu_custom_call" | custom-call | tf_op jit(solution)/shard_map/project/pallas_call | solution.py:391
  118.9 83.4 %student.1 = (bf16[128,1024]{1,0:T(8,128)(2,1)}, bf16[224,1024]{1,0:T(8,128)(2,1)}, f32[16,128]{1,0:T(8,128)}) custom-call(s32[16]{0:T(128)} %len_ref.1, f32[1]{0:T(128)S(6)} %copy.13.scale_ref, bf16[6,1024,256]{2,1,0:T(8,128)(2,1)} %get-tuple-element.14.qkv_ref, bf16[4,256,3584]{2,1,0:T(8,128)(2,1)} %get-tuple-element.15.wout_hbm, ...), custom_call_target="tpu_custom_call" | custom-call | tf_op jit(solution)/shard_map/student/pallas_call | solution.py:908
  202.3 2.0 finish.1
